TPU v7x, 32 devices: a whole 2x2x4 slice. The times are simulated.
32 devices in a mesh: groups: 2 (over y), slab: 8 (over z, x), grid: 2 (over core).
Axes of the slice: x: 2, y: 2, z: 4, core: 2. Of those that a mesh axis runs over, the one named last changes fastest.
Arguments:
- grids_a: float32 [4, 3, 32, 16, 128], P(('groups', 'grid'), None, 'slab'), parts along dimension 0, may hold values from -4 to 4, as said below
- grids_b: float32 [4, 3, 64, 8, 128], P(('groups', 'grid'), None, 'slab'), parts along dimension 0, may hold values from -4 to 4, as said below
- coeffs: int32 [4], replicated, may hold values from -2 to 2
Outputs:
- out_a: float32 [4, 3, 32, 16, 128], P(('groups', 'grid'), None, 'slab'), parts along dimension 0
- out_b: float32 [4, 3, 64, 8, 128], P(('groups', 'grid'), None, 'slab'), parts along dimension 0
- combined_a: float32 [4, 3, 32, 16, 128], P(('groups', 'grid'), None, 'slab'), parts along dimension 0
- combined_b: float32 [4, 3, 64, 8, 128], P(('groups', 'grid'), None, 'slab'), parts along dimension 0
There are 2 independent parts, one for each index of `groups`. A program takes and returns all parts, laid end to end along the dimension named above; an argument that names none is the same for every part. Nothing has to cross between parts.
Inputs may be any that keep to these rules, and one draw needn't show every extreme that they name: `coeffs`: coefficients of grids_a[0], grids_a[1], grids_b[0], grids_b[1] in this order. `grids_a`: velocity components. `grids_b`: velocity components.
All inputs are finite; a program needn't handle non-finite values.
Results may differ from a plain program's by a relative error of at most 0.0003.
Values sent between devices are 32-bit elements; how exact they have to be, the bound alone decides.
A program may use at most 64 MiB of HBM per device.

v0:
```python
import math

import jax
import jax.numpy as jnp
from jax import lax
from jax.sharding import PartitionSpec as P

first_coef = (0.8, -0.2, 4.0 / 105.0, -1.0 / 280.0)
second_coef = (1.6, -0.2, 8.0 / 315.0, -1.0 / 560.0)
second_mid = -205.0 / 72.0


def shifted(block, axis, distance):
    devices = range(lax.axis_size(axis))
    route = [((i - distance) % len(devices), i) for i in devices]
    return lax.ppermute(block, axis, route)


def extended_2(block, sides, width):
    for axis, dim in sides:
        count = lax.axis_size(axis)
        forward = [(i, i + 1) for i in range(count - 1)]
        forward.append((count - 1, 0))
        backward = [(target, source) for source, target in forward]
        low = lax.ppermute(
            lax.slice_in_dim(block, block.shape[dim] - width, None, axis=dim), axis, forward
        )
        high = lax.ppermute(lax.slice_in_dim(block, 0, width, axis=dim), axis, backward)
        block = jnp.concatenate([low, block, high], axis=dim)
    return block


def partner_2(value, axis, apart):
    mask = 2**apart
    pairs = [(source, source ^ mask) for source in range(lax.axis_size(axis))]
    return lax.ppermute(value, axis, pairs)


def periodic_terms(values, dimension, spacing):
    gradient = jnp.zeros_like(values)
    curvature = second_mid * values
    for offset in range(1, 5):
        forward = jnp.roll(values, -offset, dimension)
        behind = jnp.roll(values, offset, dimension)
        gradient = gradient + first_coef[offset - 1] * (forward - behind)
        curvature = curvature + second_coef[offset - 1] * (forward + behind)
    return (gradient / spacing, curvature / (spacing * spacing))


def slab_rate(values, padded, spacings, viscosity):
    depth = values.shape[1]
    z_grad = jnp.zeros_like(values)
    z_curv = second_mid * values
    for offset in range(1, 5):
        forward = padded[:, 4 + offset : 4 + offset + depth]
        behind = padded[:, 4 - offset : 4 - offset + depth]
        z_grad = z_grad + first_coef[offset - 1] * (forward - behind)
        z_curv = z_curv + second_coef[offset - 1] * (forward + behind)
    z_grad = z_grad / spacings[0]
    z_curv = z_curv / (spacings[0] * spacings[0])
    y_grad, y_curv = periodic_terms(values, 2, spacings[1])
    x_grad, x_curv = periodic_terms(values, 3, spacings[2])
    carried = values[0:1] * x_grad + values[1:2] * y_grad + values[2:3] * z_grad
    return viscosity * (x_curv + y_curv + z_curv) - carried


def runge_kutta(values, tendency, time_step):
    k_one = tendency(values)
    k_two = tendency(values + 0.5 * time_step * k_one)
    k_three = tendency(values + 0.5 * time_step * k_two)
    k_four = tendency(values + time_step * k_three)
    return values + time_step / 6.0 * (k_one + 2.0 * k_two + 2.0 * k_three + k_four)


def hier_axis(values, dimension, sense):
    leading = jnp.moveaxis(values, dimension, 0)
    length = leading.shape[0]
    strides = []
    stride = 1
    while stride < length:
        strides.append(stride)
        stride = stride * 2
    if sense > 0:
        strides = strides[::-1]
    for stride in strides:
        blocks = leading.reshape((length // (2 * stride), 2 * stride) + leading.shape[1:])
        left_node = blocks[:, 0]
        right_node = jnp.roll(left_node, -1, 0)
        middle = blocks[:, stride] + sense * 0.5 * (left_node + right_node)
        blocks = blocks.at[:, stride].set(middle)
        leading = blocks.reshape(leading.shape)
    return jnp.moveaxis(leading, 0, dimension)


def level_table(length, sense):
    return hier_axis(jnp.eye(length, dtype=jnp.float32), 0, sense)


def across_rows(values, sense):
    x_table = level_table(values.shape[3], sense)
    y_table = level_table(values.shape[2], sense)
    values = jnp.einsum("czyx,wx->czyw", values, x_table, precision=lax.Precision.HIGHEST)
    return jnp.einsum("czyx,wy->czwx", values, y_table, precision=lax.Precision.HIGHEST)


def fine_z(values, next_plane, sense):
    depth = values.shape[1]
    extended = jnp.concatenate([values, next_plane[:, None]], axis=1)
    strides = []
    stride = 1
    while stride < depth:
        strides.append(stride)
        stride = stride * 2
    if sense > 0:
        strides = strides[::-1]
    for stride in strides:
        middle = extended[:, stride : depth : 2 * stride]
        left_node = extended[:, 0 : depth : 2 * stride]
        right_node = extended[:, 2 * stride : depth + 1 : 2 * stride]
        extended = extended.at[:, stride : depth : 2 * stride].set(
            middle + sense * 0.5 * (left_node + right_node)
        )
    return extended[:, :depth]


def next_of(plane):
    return shifted(plane, "slab", -1)


def move_planes(planes, distance):
    return shifted(planes, "slab", distance)


def ladder(planes, sense):
    slab_count = lax.axis_size("slab")
    position = lax.axis_index("slab")
    distances = [2**exponent for exponent in range(slab_count.bit_length() - 1)]
    if sense > 0:
        distances = distances[::-1]
    for distance in distances:
        if 2 * distance < slab_count:
            paired = planes + move_planes(planes, -2 * distance)
        else:
            paired = planes + planes
        from_left = move_planes(paired, distance)
        active = position % (2 * distance) == distance
        planes = jnp.where(active, planes + sense * 0.5 * from_left, planes)
    return planes


def coarse_levels(planes, sense):
    return ladder(planes, sense)


def to_surplus(values):
    values = across_rows(values, -1)
    values = fine_z(values, next_of(values[:, 0]), -1)
    return values.at[:, 0].set(coarse_levels(values[:, 0], -1))


def to_nodal(values):
    values = values.at[:, 0].set(coarse_levels(values[:, 0], 1))
    values = fine_z(values, next_of(values[:, 0]), 1)
    return across_rows(values, 1)


def carry_over(source, target_dims):
    result = source
    for dimension in (1, 2, 3):
        have_cells = result.shape[dimension]
        want_cells = target_dims[dimension - 1]
        common = min(have_cells, want_cells)
        result = lax.slice_in_dim(result, 0, have_cells, have_cells // common, dimension)
        factor = want_cells // common
        if factor > 1:
            spread = jnp.expand_dims(result, dimension + 1)
            widths = [(0, 0)] * spread.ndim
            widths[dimension + 1] = (0, factor - 1)
            spread = jnp.pad(spread, widths)
            new_shape = list(result.shape)
            new_shape[dimension] = want_cells
            result = spread.reshape(new_shape)
    return result


def swap_frame(values):
    turned = jnp.stack([values[1], values[0], values[2]])
    return jnp.swapaxes(turned, 2, 3)


def gather_terms(target_dims, pieces):
    summed = None
    for weight, source in pieces:
        term = weight * carry_over(source, target_dims)
        summed = term if summed is None else summed + term
    return summed


def shards(grids_a, grids_b, coeffs):
    own_a = grids_a[0]
    own_b = grids_b[0]
    slab_count = lax.axis_size("slab")
    x_cells = own_a.shape[3]
    za_cells = own_a.shape[1] * slab_count
    zb_cells = own_b.shape[1] * slab_count
    finest = 2.0 * math.pi / max(x_cells, 2 * za_cells)
    time_step = 0.1 * finest
    viscosity = 0.2 * finest
    spacing_a = (2.0 * math.pi / za_cells, 2.0 * math.pi / own_a.shape[2], 2.0 * math.pi / x_cells)
    spacing_b = (2.0 * math.pi / zb_cells, 2.0 * math.pi / own_b.shape[2], 2.0 * math.pi / x_cells)

    def rim_a(values):
        return extended_2(values, (("slab", 1),), 4)

    def rim_b(values):
        return extended_2(values, (("slab", 1),), 4)

    moved_a = runge_kutta(own_a, lambda v: slab_rate(v, rim_a(v), spacing_a, viscosity), time_step)
    moved_b = runge_kutta(own_b, lambda v: slab_rate(v, rim_b(v), spacing_b, viscosity), time_step)
    surplus_a = to_surplus(moved_a)
    surplus_b = to_surplus(moved_b)
    member = lax.axis_index("grid")
    partner = 1 - member
    weights = coeffs.astype(jnp.float32)
    view_a = swap_frame(surplus_a)
    view_b = swap_frame(surplus_b)
    packed = jnp.concatenate([view_a.reshape(-1), view_b.reshape(-1)])
    received = partner_2(packed, "grid", 0)
    got_a = received[: view_a.size].reshape(view_a.shape)
    got_b = received[view_a.size :].reshape(view_b.shape)
    pieces = [
        (weights[member], surplus_a),
        (weights[2 + member], surplus_b),
        (weights[partner], got_a),
        (weights[2 + partner], got_b),
    ]
    joined_a = gather_terms(surplus_a.shape[1:], pieces)
    joined_b = gather_terms(surplus_b.shape[1:], pieces)
    return (to_nodal(joined_a)[None], to_nodal(joined_b)[None], joined_a[None], joined_b[None])


def solution(mesh):
    placed = (
        P(("groups", "grid"), None, "slab", None, None),
        P(("groups", "grid"), None, "slab", None, None),
        P(),
    )
    return jax.shard_map(
        shards,
        mesh=mesh,
        in_specs=placed,
        out_specs=(
            P(("groups", "grid"), None, "slab", None, None),
            P(("groups", "grid"), None, "slab", None, None),
            P(("groups", "grid"), None, "slab", None, None),
            P(("groups", "grid"), None, "slab", None, None),
        ),
        check_vma=False,
    )
```

profile of v0, /device:TPU:0, one launch (start us, length us, event | category | flops | bytes accessed | tf_op | source)
XLA Modules:
  0.0 219.0 jit_solution(1486672426591824980)
XLA Ops:
  0.6 6.0 %collective-permute-start = (f32[3,4,16,128]{3,2,1,0:T(8,128)}, f32[3,4,16,128]{3,2,1,0:T(8,128)}, u32[]{:S(2)}, u32[]{:S(2)}) collective-permute-start(f32[3,4,16,128]{3,2,1,0:T(8,128)} %bitcast.271), channel_id=1, source_target_pairs={{2,0},{4,2},{6,4},{8,6},{10,8},{12,10},{14,12},{0,14},{3,1},{5,3},... | collective-permute-start | bytes 294920 | tf_op jit(solution)/shard_map/ppermute | solution.py:28
  6.7 1.5 fusion.552
  8.2 4.7 %collective-permute-start.14 = (f32[3,4,8,128]{3,2,1,0:T(8,128)}, f32[3,4,8,128]{3,2,1,0:T(8,128)}, u32[]{:S(2)}, u32[]{:S(2)}) collective-permute-start(f32[3,4,8,128]{3,2,1,0:T(8,128)} %get-tuple-element.870), channel_id=1, source_target_pairs={{2,0},{4,2},{6,4},{8,6},{10,8},{12,10},{14,12},{0,14},{3,1},{5,3},... | collective-permute-start | bytes 147464 | tf_op jit(solution)/shard_map/ppermute | solution.py:28
  42.6 1.2 fusion.360
  46.2 1.3 fusion.362
  49.9 1.2 fusion.358
  54.1 1.4 fusion.295
  55.5 1.3 fusion.349
  59.9 2.3 %multiply_add_fusion.5 = (f32[3,8,8,128]{3,2,1,0:T(8,128)S(1)}, f32[3,8,8,128]{3,2,1,0:T(8,128)S(1)}) fusion(f32[1,3,8,8,128]{4,3,2,1,0:T(8,128)S(1)} %copy-done, f32[8,8,128]{2,1,0:T(8,128)} %get-tuple-element.873, f32[8,8,128]{2,1,0:T(8,128)} %get-tuple-element.874, f32[8,8,128]{2,1,0:T(8,128)} %get-tuple-element.872, f32[3,8,8,128]{3,2,1,0:T(8,128)S(1)} %bitcast.270, ...), kind=kLoop, calls=%fused_computation.392 | loop fusion | flops 2629632 | bytes 2064384 | tf_op jit(solution)/shard_map/add | solution.py:69
  63.3 4.8 %collective-permute-start.16 = (f32[3,4,8,128]{3,2,1,0:T(8,128)S(1)}, f32[3,4,8,128]{3,2,1,0:T(8,128)S(1)}, u32[]{:S(2)}, u32[]{:S(2)}) collective-permute-start(f32[3,4,8,128]{3,2,1,0:T(8,128)S(1)} %get-tuple-element.835), channel_id=1, source_target_pairs={{2,0},{4,2},{6,4},{8,6},{10,8},{12,10},{14,12},{0,14},{3,1},{5,3},... | collective-permute-start | bytes 147464 | tf_op jit(solution)/shard_map/ppermute | solution.py:28
  68.2 1.7 multiply_add_fusion.12
  70.8 4.8 %collective-permute-start.2 = (f32[3,4,16,128]{3,2,1,0:T(8,128)S(1)}, f32[3,4,16,128]{3,2,1,0:T(8,128)S(1)}, u32[]{:S(2)}, u32[]{:S(2)}) collective-permute-start(f32[3,4,16,128]{3,2,1,0:T(8,128)S(1)} %get-tuple-element.576), channel_id=1, source_target_pairs={{2,0},{4,2},{6,4},{8,6},{10,8},{12,10},{14,12},{0,14},{3,1},{5,3},... | collective-permute-start | bytes 294920 | tf_op jit(solution)/shard_map/ppermute | solution.py:28
  77.2 4.8 %collective-permute-start.18 = (f32[3,4,8,128]{3,2,1,0:T(8,128)S(1)}, f32[3,4,8,128]{3,2,1,0:T(8,128)S(1)}, u32[]{:S(2)}, u32[]{:S(2)}) collective-permute-start(f32[3,4,8,128]{3,2,1,0:T(8,128)S(1)} %get-tuple-element.800), channel_id=1, source_target_pairs={{2,0},{4,2},{6,4},{8,6},{10,8},{12,10},{14,12},{0,14},{3,1},{5,3},... | collective-permute-start | bytes 147464 | tf_op jit(solution)/shard_map/ppermute | solution.py:28
  82.0 1.7 collective-permute-done.18
  83.7 5.0 %collective-permute-done.19 = f32[3,4,8,128]{3,2,1,0:T(8,128)S(1)} collective-permute-done((f32[3,4,8,128]{3,2,1,0:T(8,128)S(1)}, f32[3,4,8,128]{3,2,1,0:T(8,128)S(1)}, u32[]{:S(2)}, u32[]{:S(2)}) %collective-permute-start.19) | collective-permute-done | bytes 49184 | tf_op jit(solution)/shard_map/ppermute | solution.py:25
  90.4 2.0 collective-permute-start.21
  93.8 2.8 %collective-permute-start.4 = (f32[3,4,16,128]{3,2,1,0:T(8,128)S(1)}, f32[3,4,16,128]{3,2,1,0:T(8,128)S(1)}, u32[]{:S(2)}, u32[]{:S(2)}) collective-permute-start(f32[3,4,16,128]{3,2,1,0:T(8,128)S(1)} %get-tuple-element.574), channel_id=1, source_target_pairs={{2,0},{4,2},{6,4},{8,6},{10,8},{12,10},{14,12},{0,14},{3,1},{5,3},... | collective-permute-start | bytes 294920 | tf_op jit(solution)/shard_map/ppermute | solution.py:28
  98.3 4.3 %collective-permute-start.22 = (f32[3,8,128]{2,1,0:T(8,128)S(1)}, f32[3,8,128]{2,1,0:T(8,128)S(1)}, u32[]{:S(2)}, u32[]{:S(2)}) collective-permute-start(f32[3,8,128]{2,1,0:T(8,128)S(1)} %slice_bitcast_fusion.6), channel_id=1, source_target_pairs={{2,0},{4,2},{6,4},{8,6},{10,8},{12,10},{14,12},{0,14},{3,1},{5,3},... | collective-permute-start | bytes 36872 | tf_op jit(solution)/shard_map/ppermute | solution.py:16
  102.6 1.4 collective-permute-done.22
  106.4 2.8 %collective-permute-done.23 = f32[3,8,128]{2,1,0:T(8,128)S(1)} collective-permute-done((f32[3,8,128]{2,1,0:T(8,128)S(1)}, f32[3,8,128]{2,1,0:T(8,128)S(1)}, u32[]{:S(2)}, u32[]{:S(2)}) %collective-permute-start.23) | collective-permute-done | bytes 12320 | tf_op jit(solution)/shard_map/ppermute | solution.py:16
  109.2 3.3 %collective-permute-start.24 = (f32[3,8,128]{2,1,0:T(8,128)S(1)}, f32[3,8,128]{2,1,0:T(8,128)S(1)}, u32[]{:S(2)}, u32[]{:S(2)}) collective-permute-start(f32[3,8,128]{2,1,0:T(8,128)S(1)} %fusion.419), channel_id=1, source_target_pairs={{14,0},{0,2},{2,4},{4,6},{6,8},{8,10},{10,12},{12,14},{15,1},{1,3}... | collective-permute-start | bytes 36872 | tf_op jit(solution)/shard_map/ppermute | solution.py:16
  112.5 1.6 multiply_add_fusion.8
  114.9 3.8 %collective-permute-start.6 = (f32[3,4,16,128]{3,2,1,0:T(8,128)S(1)}, f32[3,4,16,128]{3,2,1,0:T(8,128)S(1)}, u32[]{:S(2)}, u32[]{:S(2)}) collective-permute-start(f32[3,4,16,128]{3,2,1,0:T(8,128)S(1)} %get-tuple-element.572), channel_id=1, source_target_pairs={{2,0},{4,2},{6,4},{8,6},{10,8},{12,10},{14,12},{0,14},{3,1},{5,3},... | collective-permute-start | bytes 294920 | tf_op jit(solution)/shard_map/ppermute | solution.py:28
  118.8 2.2 %collective-permute-done.6 = f32[3,4,16,128]{3,2,1,0:T(8,128)S(1)} collective-permute-done((f32[3,4,16,128]{3,2,1,0:T(8,128)S(1)}, f32[3,4,16,128]{3,2,1,0:T(8,128)S(1)}, u32[]{:S(2)}, u32[]{:S(2)}) %collective-permute-start.6) | collective-permute-done | bytes 98336 | tf_op jit(solution)/shard_map/ppermute | solution.py:28
  121.0 5.0 %collective-permute-done.7 = f32[3,4,16,128]{3,2,1,0:T(8,128)S(1)} collective-permute-done((f32[3,4,16,128]{3,2,1,0:T(8,128)S(1)}, f32[3,4,16,128]{3,2,1,0:T(8,128)S(1)}, u32[]{:S(2)}, u32[]{:S(2)}) %collective-permute-start.7) | collective-permute-done | bytes 98336 | tf_op jit(solution)/shard_map/ppermute | solution.py:25
  127.8 3.2 %collective-permute-done.8 = f32[3,16,128]{2,1,0:T(8,128)S(1)} collective-permute-done((f32[3,16,128]{2,1,0:T(8,128)S(1)}, f32[3,16,128]{2,1,0:T(8,128)S(1)}, u32[]{:S(2)}, u32[]{:S(2)}) %collective-permute-start.8) | collective-permute-done | bytes 24608 | tf_op jit(solution)/shard_map/ppermute | solution.py:16
  132.6 2.0 collective-permute-start.26
  135.6 1.5 collective-permute-start.10
  138.1 4.3 %collective-permute-done.10 = f32[3,16,128]{2,1,0:T(8,128)S(1)} collective-permute-done((f32[3,16,128]{2,1,0:T(8,128)S(1)}, f32[3,16,128]{2,1,0:T(8,128)S(1)}, u32[]{:S(2)}, u32[]{:S(2)}) %collective-permute-start.10) | collective-permute-done | bytes 24608 | tf_op jit(solution)/shard_map/ppermute | solution.py:16
  142.7 4.5 %collective-permute-done.11 = f32[3,16,128]{2,1,0:T(8,128)S(1)} collective-permute-done((f32[3,16,128]{2,1,0:T(8,128)S(1)}, f32[3,16,128]{2,1,0:T(8,128)S(1)}, u32[]{:S(2)}, u32[]{:S(2)}) %collective-permute-start.11) | collective-permute-done | bytes 24608 | tf_op jit(solution)/shard_map/ppermute | solution.py:16
  147.2 5.6 %collective-permute-done.12 = f32[3,16,128]{2,1,0:T(8,128)S(1)} collective-permute-done((f32[3,16,128]{2,1,0:T(8,128)S(1)}, f32[3,16,128]{2,1,0:T(8,128)S(1)}, u32[]{:S(2)}, u32[]{:S(2)}) %collective-permute-start.12) | collective-permute-done | bytes 24608 | tf_op jit(solution)/shard_map/ppermute | solution.py:16
  154.2 3.4 %collective-permute-done.13 = f32[3,16,128]{2,1,0:T(8,128)S(1)} collective-permute-done((f32[3,16,128]{2,1,0:T(8,128)S(1)}, f32[3,16,128]{2,1,0:T(8,128)S(1)}, u32[]{:S(2)}, u32[]{:S(2)}) %collective-permute-start.13) | collective-permute-done | bytes 24608 | tf_op jit(solution)/shard_map/ppermute | solution.py:16
  159.7 1.3 slice.3199
  161.8 1.4 slice.3202
  167.7 1.2 copy.123
  169.8 1.3 fusion.42
  171.2 2.0 slice.3155
  175.9 3.0 %collective-permute-start.36 = (f32[3,8,128]{2,1,0:T(8,128)S(1)}, f32[3,8,128]{2,1,0:T(8,128)S(1)}, u32[]{:S(2)}, u32[]{:S(2)}) collective-permute-start(f32[3,8,128]{2,1,0:T(8,128)S(1)} %add_select_fusion.8), channel_id=1, source_target_pairs={{8,0},{10,2},{12,4},{14,6},{0,8},{2,10},{4,12},{6,14},{9,1},{11,3}... | collective-permute-start | bytes 36872 | tf_op jit(solution)/shard_map/ppermute | solution.py:16
  180.8 2.8 %collective-permute-start.29 = (f32[3,16,128]{2,1,0:T(8,128)S(1)}, f32[3,16,128]{2,1,0:T(8,128)S(1)}, u32[]{:S(2)}, u32[]{:S(2)}) collective-permute-start(f32[3,16,128]{2,1,0:T(8,128)S(1)} %fusion.324), channel_id=1, source_target_pairs={{8,0},{10,2},{12,4},{14,6},{0,8},{2,10},{4,12},{6,14},{9,1},{11,3}... | collective-permute-start | bytes 73736 | tf_op jit(solution)/shard_map/ppermute | solution.py:16
  183.6 2.6 %collective-permute-done.37 = f32[3,8,128]{2,1,0:T(8,128)S(1)} collective-permute-done((f32[3,8,128]{2,1,0:T(8,128)S(1)}, f32[3,8,128]{2,1,0:T(8,128)S(1)}, u32[]{:S(2)}, u32[]{:S(2)}) %collective-permute-start.37) | collective-permute-done | bytes 12320 | tf_op jit(solution)/shard_map/ppermute | solution.py:16
  187.3 2.6 %collective-permute-done.38 = f32[3,8,128]{2,1,0:T(8,128)S(1)} collective-permute-done((f32[3,8,128]{2,1,0:T(8,128)S(1)}, f32[3,8,128]{2,1,0:T(8,128)S(1)}, u32[]{:S(2)}, u32[]{:S(2)}) %collective-permute-start.38) | collective-permute-done | bytes 12320 | tf_op jit(solution)/shard_map/ppermute | solution.py:16
  191.0 5.3 %collective-permute-done.39 = f32[3,8,128]{2,1,0:T(8,128)S(1)} collective-permute-done((f32[3,8,128]{2,1,0:T(8,128)S(1)}, f32[3,8,128]{2,1,0:T(8,128)S(1)}, u32[]{:S(2)}, u32[]{:S(2)}) %collective-permute-start.39) | collective-permute-done | bytes 12320 | tf_op jit(solution)/shard_map/ppermute | solution.py:16
  197.3 2.7 %collective-permute-done.40 = f32[3,8,128]{2,1,0:T(8,128)S(1)} collective-permute-done((f32[3,8,128]{2,1,0:T(8,128)S(1)}, f32[3,8,128]{2,1,0:T(8,128)S(1)}, u32[]{:S(2)}, u32[]{:S(2)}) %collective-permute-start.40) | collective-permute-done | bytes 12320 | tf_op jit(solution)/shard_map/ppermute | solution.py:16
  200.1 2.9 %collective-permute-done.31 = f32[3,16,128]{2,1,0:T(8,128)S(1)} collective-permute-done((f32[3,16,128]{2,1,0:T(8,128)S(1)}, f32[3,16,128]{2,1,0:T(8,128)S(1)}, u32[]{:S(2)}, u32[]{:S(2)}) %collective-permute-start.31) | collective-permute-done | bytes 24608 | tf_op jit(solution)/shard_map/ppermute | solution.py:16
  204.4 2.4 %collective-permute-done.32 = f32[3,16,128]{2,1,0:T(8,128)S(1)} collective-permute-done((f32[3,16,128]{2,1,0:T(8,128)S(1)}, f32[3,16,128]{2,1,0:T(8,128)S(1)}, u32[]{:S(2)}, u32[]{:S(2)}) %collective-permute-start.32) | collective-permute-done | bytes 24608 | tf_op jit(solution)/shard_map/ppermute | solution.py:16
  206.8 2.0 collective-permute-start.33
  209.0 4.2 %collective-permute-done.33 = f32[3,16,128]{2,1,0:T(8,128)S(1)} collective-permute-done((f32[3,16,128]{2,1,0:T(8,128)S(1)}, f32[3,16,128]{2,1,0:T(8,128)S(1)}, u32[]{:S(2)}, u32[]{:S(2)}) %collective-permute-start.33) | collective-permute-done | bytes 24608 | tf_op jit(solution)/shard_map/ppermute | solution.py:16
  214.8 2.4 %collective-permute-done.34 = f32[3,16,128]{2,1,0:T(8,128)S(1)} collective-permute-done((f32[3,16,128]{2,1,0:T(8,128)S(1)}, f32[3,16,128]{2,1,0:T(8,128)S(1)}, u32[]{:S(2)}, u32[]{:S(2)}) %collective-permute-start.34) | collective-permute-done | bytes 24608 | tf_op jit(solution)/shard_map/ppermute | solution.py:16
  (438 shorter events, 78.9 us)
Async XLA Ops:
  0.6 16.5 %copy-start.1 = (f32[1,3,4,16,128]{4,3,2,1,0:T(8,128)S(1)}, f32[1,3,4,16,128]{4,3,2,1,0:T(8,128)}, u32[]{:S(2)}) copy-start(f32[1,3,4,16,128]{4,3,2,1,0:T(8,128)} %param.103) | copy-start | bytes 294916
  0.6 67.4 %collective-permute-start = (f32[3,4,16,128]{3,2,1,0:T(8,128)}, f32[3,4,16,128]{3,2,1,0:T(8,128)}, u32[]{:S(2)}, u32[]{:S(2)}) collective-permute-start(f32[3,4,16,128]{3,2,1,0:T(8,128)} %bitcast.271), channel_id=1, source_target_pairs={{2,0},{4,2},{6,4},{8,6},{10,8},{12,10},{14,12},{0,14},{3,1},{5,3},... | collective-permute-start | bytes 294920 | tf_op jit(solution)/shard_map/ppermute | solution.py:28
  6.7 61.4 %collective-permute-start.1 = (f32[3,4,16,128]{3,2,1,0:T(8,128)}, f32[3,4,16,128]{3,2,1,0:T(8,128)}, u32[]{:S(2)}, u32[]{:S(2)}) collective-permute-start(f32[3,4,16,128]{3,2,1,0:T(8,128)} %bitcast.272), channel_id=1, source_target_pairs={{0,2},{2,4},{4,6},{6,8},{8,10},{10,12},{12,14},{14,0},{1,3},{3,5},... | collective-permute-start | bytes 294920 | tf_op jit(solution)/shard_map/ppermute | solution.py:25
  8.2 51.8 %collective-permute-start.14 = (f32[3,4,8,128]{3,2,1,0:T(8,128)}, f32[3,4,8,128]{3,2,1,0:T(8,128)}, u32[]{:S(2)}, u32[]{:S(2)}) collective-permute-start(f32[3,4,8,128]{3,2,1,0:T(8,128)} %get-tuple-element.870), channel_id=1, source_target_pairs={{2,0},{4,2},{6,4},{8,6},{10,8},{12,10},{14,12},{0,14},{3,1},{5,3},... | collective-permute-start | bytes 147464 | tf_op jit(solution)/shard_map/ppermute | solution.py:28
  12.9 47.1 %collective-permute-start.15 = (f32[3,4,8,128]{3,2,1,0:T(8,128)}, f32[3,4,8,128]{3,2,1,0:T(8,128)}, u32[]{:S(2)}, u32[]{:S(2)}) collective-permute-start(f32[3,4,8,128]{3,2,1,0:T(8,128)} %get-tuple-element.871), channel_id=1, source_target_pairs={{0,2},{2,4},{4,6},{6,8},{8,10},{10,12},{12,14},{14,0},{1,3},{3,5},... | collective-permute-start | bytes 147464 | tf_op jit(solution)/shard_map/ppermute | solution.py:25
  17.4 6.9 %copy-start = (f32[1,3,8,8,128]{4,3,2,1,0:T(8,128)S(1)}, f32[1,3,8,8,128]{4,3,2,1,0:T(8,128)}, u32[]{:S(2)}) copy-start(f32[1,3,8,8,128]{4,3,2,1,0:T(8,128)} %param.104) | copy-start | bytes 294916
  63.3 12.3 %collective-permute-start.16 = (f32[3,4,8,128]{3,2,1,0:T(8,128)S(1)}, f32[3,4,8,128]{3,2,1,0:T(8,128)S(1)}, u32[]{:S(2)}, u32[]{:S(2)}) collective-permute-start(f32[3,4,8,128]{3,2,1,0:T(8,128)S(1)} %get-tuple-element.835), channel_id=1, source_target_pairs={{2,0},{4,2},{6,4},{8,6},{10,8},{12,10},{14,12},{0,14},{3,1},{5,3},... | collective-permute-start | bytes 147464 | tf_op jit(solution)/shard_map/ppermute | solution.py:28
  68.0 7.6 %collective-permute-start.17 = (f32[3,4,8,128]{3,2,1,0:T(8,128)S(1)}, f32[3,4,8,128]{3,2,1,0:T(8,128)S(1)}, u32[]{:S(2)}, u32[]{:S(2)}) collective-permute-start(f32[3,4,8,128]{3,2,1,0:T(8,128)S(1)} %get-tuple-element.836), channel_id=1, source_target_pairs={{0,2},{2,4},{4,6},{6,8},{8,10},{10,12},{12,14},{14,0},{1,3},{3,5},... | collective-permute-start | bytes 147464 | tf_op jit(solution)/shard_map/ppermute | solution.py:25
  70.8 21.6 %collective-permute-start.2 = (f32[3,4,16,128]{3,2,1,0:T(8,128)S(1)}, f32[3,4,16,128]{3,2,1,0:T(8,128)S(1)}, u32[]{:S(2)}, u32[]{:S(2)}) collective-permute-start(f32[3,4,16,128]{3,2,1,0:T(8,128)S(1)} %get-tuple-element.576), channel_id=1, source_target_pairs={{2,0},{4,2},{6,4},{8,6},{10,8},{12,10},{14,12},{0,14},{3,1},{5,3},... | collective-permute-start | bytes 294920 | tf_op jit(solution)/shard_map/ppermute | solution.py:28
  75.6 16.8 %collective-permute-start.3 = (f32[3,4,16,128]{3,2,1,0:T(8,128)S(1)}, f32[3,4,16,128]{3,2,1,0:T(8,128)S(1)}, u32[]{:S(2)}, u32[]{:S(2)}) collective-permute-start(f32[3,4,16,128]{3,2,1,0:T(8,128)S(1)} %get-tuple-element.576), channel_id=1, source_target_pairs={{0,2},{2,4},{4,6},{6,8},{8,10},{10,12},{12,14},{14,0},{1,3},{3,5},... | collective-permute-start | bytes 294920 | tf_op jit(solution)/shard_map/ppermute | solution.py:25
  77.2 6.5 %collective-permute-start.18 = (f32[3,4,8,128]{3,2,1,0:T(8,128)S(1)}, f32[3,4,8,128]{3,2,1,0:T(8,128)S(1)}, u32[]{:S(2)}, u32[]{:S(2)}) collective-permute-start(f32[3,4,8,128]{3,2,1,0:T(8,128)S(1)} %get-tuple-element.800), channel_id=1, source_target_pairs={{2,0},{4,2},{6,4},{8,6},{10,8},{12,10},{14,12},{0,14},{3,1},{5,3},... | collective-permute-start | bytes 147464 | tf_op jit(solution)/shard_map/ppermute | solution.py:28
  81.9 6.8 %collective-permute-start.19 = (f32[3,4,8,128]{3,2,1,0:T(8,128)S(1)}, f32[3,4,8,128]{3,2,1,0:T(8,128)S(1)}, u32[]{:S(2)}, u32[]{:S(2)}) collective-permute-start(f32[3,4,8,128]{3,2,1,0:T(8,128)S(1)} %get-tuple-element.801), channel_id=1, source_target_pairs={{0,2},{2,4},{4,6},{6,8},{8,10},{10,12},{12,14},{14,0},{1,3},{3,5},... | collective-permute-start | bytes 147464 | tf_op jit(solution)/shard_map/ppermute | solution.py:25
  90.3 6.4 %collective-permute-start.20 = (f32[3,4,8,128]{3,2,1,0:T(8,128)S(1)}, f32[3,4,8,128]{3,2,1,0:T(8,128)S(1)}, u32[]{:S(2)}, u32[]{:S(2)}) collective-permute-start(f32[3,4,8,128]{3,2,1,0:T(8,128)S(1)} %get-tuple-element.769), channel_id=1, source_target_pairs={{2,0},{4,2},{6,4},{8,6},{10,8},{12,10},{14,12},{0,14},{3,1},{5,3},... | collective-permute-start | bytes 147464 | tf_op jit(solution)/shard_map/ppermute | solution.py:28
  90.4 6.8 %collective-permute-start.21 = (f32[3,4,8,128]{3,2,1,0:T(8,128)S(1)}, f32[3,4,8,128]{3,2,1,0:T(8,128)S(1)}, u32[]{:S(2)}, u32[]{:S(2)}) collective-permute-start(f32[3,4,8,128]{3,2,1,0:T(8,128)S(1)} %get-tuple-element.768), channel_id=1, source_target_pairs={{0,2},{2,4},{4,6},{6,8},{8,10},{10,12},{12,14},{14,0},{1,3},{3,5},... | collective-permute-start | bytes 147464 | tf_op jit(solution)/shard_map/ppermute | solution.py:25
  93.8 18.7 %collective-permute-start.4 = (f32[3,4,16,128]{3,2,1,0:T(8,128)S(1)}, f32[3,4,16,128]{3,2,1,0:T(8,128)S(1)}, u32[]{:S(2)}, u32[]{:S(2)}) collective-permute-start(f32[3,4,16,128]{3,2,1,0:T(8,128)S(1)} %get-tuple-element.574), channel_id=1, source_target_pairs={{2,0},{4,2},{6,4},{8,6},{10,8},{12,10},{14,12},{0,14},{3,1},{5,3},... | collective-permute-start | bytes 294920 | tf_op jit(solution)/shard_map/ppermute | solution.py:28
  96.6 15.9 %collective-permute-start.5 = (f32[3,4,16,128]{3,2,1,0:T(8,128)S(1)}, f32[3,4,16,128]{3,2,1,0:T(8,128)}, u32[]{:S(2)}, u32[]{:S(2)}) collective-permute-start(f32[3,4,16,128]{3,2,1,0:T(8,128)S(1)} %get-tuple-element.574), channel_id=1, source_target_pairs={{0,2},{2,4},{4,6},{6,8},{8,10},{10,12},{12,14},{14,0},{1,3},{3,5},... | collective-permute-start | bytes 294920 | tf_op jit(solution)/shard_map/ppermute | solution.py:25
  97.2 6.8 %copy-start.18 = (s32[4]{0:T(128)S(1)}, s32[4]{0:T(128)}, u32[]{:S(2)}) copy-start(s32[4]{0:T(128)} %add_bitcast_fusion.6) | copy-start | bytes 52
  97.2 7.6 %copy-start.19 = (s32[2]{0:T(128)S(1)}, s32[2]{0:T(128)}, u32[]{:S(2)}) copy-start(s32[2]{0:T(128)} %add_bitcast_fusion.5) | copy-start | bytes 28
  98.3 5.7 %collective-permute-start.22 = (f32[3,8,128]{2,1,0:T(8,128)S(1)}, f32[3,8,128]{2,1,0:T(8,128)S(1)}, u32[]{:S(2)}, u32[]{:S(2)}) collective-permute-start(f32[3,8,128]{2,1,0:T(8,128)S(1)} %slice_bitcast_fusion.6), channel_id=1, source_target_pairs={{2,0},{4,2},{6,4},{8,6},{10,8},{12,10},{14,12},{0,14},{3,1},{5,3},... | collective-permute-start | bytes 36872 | tf_op jit(solution)/shard_map/ppermute | solution.py:16
  105.5 3.7 %collective-permute-start.23 = (f32[3,8,128]{2,1,0:T(8,128)S(1)}, f32[3,8,128]{2,1,0:T(8,128)S(1)}, u32[]{:S(2)}, u32[]{:S(2)}) collective-permute-start(f32[3,8,128]{2,1,0:T(8,128)S(1)} %slice_bitcast_fusion.5), channel_id=1, source_target_pairs={{4,0},{6,2},{8,4},{10,6},{12,8},{14,10},{0,12},{2,14},{5,1},{7,3},... | collective-permute-start | bytes 36872 | tf_op jit(solution)/shard_map/ppermute | solution.py:16
  109.2 18.5 %collective-permute-start.24 = (f32[3,8,128]{2,1,0:T(8,128)S(1)}, f32[3,8,128]{2,1,0:T(8,128)S(1)}, u32[]{:S(2)}, u32[]{:S(2)}) collective-permute-start(f32[3,8,128]{2,1,0:T(8,128)S(1)} %fusion.419), channel_id=1, source_target_pairs={{14,0},{0,2},{2,4},{4,6},{6,8},{8,10},{10,12},{12,14},{15,1},{1,3}... | collective-permute-start | bytes 36872 | tf_op jit(solution)/shard_map/ppermute | solution.py:16
  114.9 6.1 %collective-permute-start.6 = (f32[3,4,16,128]{3,2,1,0:T(8,128)S(1)}, f32[3,4,16,128]{3,2,1,0:T(8,128)S(1)}, u32[]{:S(2)}, u32[]{:S(2)}) collective-permute-start(f32[3,4,16,128]{3,2,1,0:T(8,128)S(1)} %get-tuple-element.572), channel_id=1, source_target_pairs={{2,0},{4,2},{6,4},{8,6},{10,8},{12,10},{14,12},{0,14},{3,1},{5,3},... | collective-permute-start | bytes 294920 | tf_op jit(solution)/shard_map/ppermute | solution.py:28
  118.7 7.4 %collective-permute-start.7 = (f32[3,4,16,128]{3,2,1,0:T(8,128)S(1)}, f32[3,4,16,128]{3,2,1,0:T(8,128)S(1)}, u32[]{:S(2)}, u32[]{:S(2)}) collective-permute-start(f32[3,4,16,128]{3,2,1,0:T(8,128)S(1)} %get-tuple-element.572), channel_id=1, source_target_pairs={{0,2},{2,4},{4,6},{6,8},{8,10},{10,12},{12,14},{14,0},{1,3},{3,5},... | collective-permute-start | bytes 294920 | tf_op jit(solution)/shard_map/ppermute | solution.py:25
  127.1 3.9 %collective-permute-start.8 = (f32[3,16,128]{2,1,0:T(8,128)S(1)}, f32[3,16,128]{2,1,0:T(8,128)S(1)}, u32[]{:S(2)}, u32[]{:S(2)}) collective-permute-start(f32[3,16,128]{2,1,0:T(8,128)S(1)} %slice_bitcast_fusion.3), channel_id=1, source_target_pairs={{2,0},{4,2},{6,4},{8,6},{10,8},{12,10},{14,12},{0,14},{3,1},{5,3},... | collective-permute-start | bytes 73736 | tf_op jit(solution)/shard_map/ppermute | solution.py:16
  127.7 4.8 %collective-permute-start.25 = (f32[3,8,128]{2,1,0:T(8,128)S(1)}, f32[3,8,128]{2,1,0:T(8,128)S(1)}, u32[]{:S(2)}, u32[]{:S(2)}) collective-permute-start(f32[3,8,128]{2,1,0:T(8,128)S(1)} %add_select_fusion.11), channel_id=1, source_target_pairs={{8,0},{10,2},{12,4},{14,6},{0,8},{2,10},{4,12},{6,14},{9,1},{11,3}... | collective-permute-start | bytes 36872 | tf_op jit(solution)/shard_map/ppermute | solution.py:16
  131.7 3.9 %collective-permute-start.9 = (f32[3,16,128]{2,1,0:T(8,128)S(1)}, f32[3,16,128]{2,1,0:T(8,128)S(1)}, u32[]{:S(2)}, u32[]{:S(2)}) collective-permute-start(f32[3,16,128]{2,1,0:T(8,128)S(1)} %slice_bitcast_fusion.2), channel_id=1, source_target_pairs={{4,0},{6,2},{8,4},{10,6},{12,8},{14,10},{0,12},{2,14},{5,1},{7,3},... | collective-permute-start | bytes 73736 | tf_op jit(solution)/shard_map/ppermute | solution.py:16
  132.6 5.5 %collective-permute-start.26 = (f32[3,8,128]{2,1,0:T(8,128)S(1)}, f32[3,8,128]{2,1,0:T(8,128)S(1)}, u32[]{:S(2)}, u32[]{:S(2)}) collective-permute-start(f32[3,8,128]{2,1,0:T(8,128)S(1)} %add.1987), channel_id=1, source_target_pairs={{12,0},{14,2},{0,4},{2,6},{4,8},{6,10},{8,12},{10,14},{13,1},{15,3... | collective-permute-start | bytes 36872 | tf_op jit(solution)/shard_map/ppermute | solution.py:16
  135.6 6.8 %collective-permute-start.10 = (f32[3,16,128]{2,1,0:T(8,128)S(1)}, f32[3,16,128]{2,1,0:T(8,128)S(1)}, u32[]{:S(2)}, u32[]{:S(2)}) collective-permute-start(f32[3,16,128]{2,1,0:T(8,128)S(1)} %fusion.420), channel_id=1, source_target_pairs={{14,0},{0,2},{2,4},{4,6},{6,8},{8,10},{10,12},{12,14},{15,1},{1,3}... | collective-permute-start | bytes 73736 | tf_op jit(solution)/shard_map/ppermute | solution.py:16
  138.1 4.6 %collective-permute-start.27 = (f32[3,8,128]{2,1,0:T(8,128)S(1)}, f32[3,8,128]{2,1,0:T(8,128)S(1)}, u32[]{:S(2)}, u32[]{:S(2)}) collective-permute-start(f32[3,8,128]{2,1,0:T(8,128)S(1)} %fusion.352), channel_id=1, source_target_pairs={{8,0},{10,2},{12,4},{14,6},{0,8},{2,10},{4,12},{6,14},{9,1},{11,3}... | collective-permute-start | bytes 36872 | tf_op jit(solution)/shard_map/ppermute | solution.py:16
  142.5 4.7 %collective-permute-start.11 = (f32[3,16,128]{2,1,0:T(8,128)S(1)}, f32[3,16,128]{2,1,0:T(8,128)S(1)}, u32[]{:S(2)}, u32[]{:S(2)}) collective-permute-start(f32[3,16,128]{2,1,0:T(8,128)S(1)} %add_select_fusion.5), channel_id=1, source_target_pairs={{8,0},{10,2},{12,4},{14,6},{0,8},{2,10},{4,12},{6,14},{9,1},{11,3}... | collective-permute-start | bytes 73736 | tf_op jit(solution)/shard_map/ppermute | solution.py:16
  147.2 5.6 %collective-permute-start.12 = (f32[3,16,128]{2,1,0:T(8,128)S(1)}, f32[3,16,128]{2,1,0:T(8,128)S(1)}, u32[]{:S(2)}, u32[]{:S(2)}) collective-permute-start(f32[3,16,128]{2,1,0:T(8,128)S(1)} %add.1809), channel_id=1, source_target_pairs={{12,0},{14,2},{0,4},{2,6},{4,8},{6,10},{8,12},{10,14},{13,1},{15,3... | collective-permute-start | bytes 73736 | tf_op jit(solution)/shard_map/ppermute | solution.py:16
  152.8 4.8 %collective-permute-start.13 = (f32[3,16,128]{2,1,0:T(8,128)S(1)}, f32[3,16,128]{2,1,0:T(8,128)S(1)}, u32[]{:S(2)}, u32[]{:S(2)}) collective-permute-start(f32[3,16,128]{2,1,0:T(8,128)S(1)} %fusion.341), channel_id=1, source_target_pairs={{8,0},{10,2},{12,4},{14,6},{0,8},{2,10},{4,12},{6,14},{9,1},{11,3}... | collective-permute-start | bytes 73736 | tf_op jit(solution)/shard_map/ppermute | solution.py:16
  158.2 2.7 %collective-permute-start.28 = (f32[49152]{0:T(1024)S(1)}, f32[49152]{0:T(1024)S(1)}, u32[]{:S(2)}, u32[]{:S(2)}) collective-permute-start(f32[49152]{0:T(1024)S(1)} %pad_maximum_fusion), channel_id=1, source_target_pairs={{0,1},{1,0},{2,3},{3,2},{4,5},{5,4},{6,7},{7,6},{8,9},{9,8},{10,11... | collective-permute-start | bytes 589832 | tf_op jit(solution)/shard_map/ppermute | solution.py:36
  171.1 4.8 %collective-permute-start.35 = (f32[3,8,128]{2,1,0:T(8,128)S(1)}, f32[3,8,128]{2,1,0:T(8,128)S(1)}, u32[]{:S(2)}, u32[]{:S(2)}) collective-permute-start(f32[3,8,128]{2,1,0:T(8,128)S(1)} %fusion.334), channel_id=1, source_target_pairs={{8,0},{10,2},{12,4},{14,6},{0,8},{2,10},{4,12},{6,14},{9,1},{11,3}... | collective-permute-start | bytes 36872 | tf_op jit(solution)/shard_map/ppermute | solution.py:16
  175.4 21.0 %copy-start.8 = (f32[64,1,128]{2,1,0:T(1,128)S(1)}, f32[64,1,128]{2,1,0:T(1,128)}, u32[]{:S(2)}) copy-start(f32[64,1,128]{2,1,0:T(1,128)} %fusion.295) | copy-start | bytes 98308
  175.4 21.2 %copy-start.16 = (f32[8,1,16]{2,1,0:T(1,128)S(1)}, f32[8,1,16]{2,1,0:T(1,128)}, u32[]{:S(2)}) copy-start(f32[8,1,16]{2,1,0:T(1,128)} %fusion.349) | copy-start | bytes 1540
  175.7 27.3 %copy-start.20 = (s32[2]{0:T(128)S(1)}, s32[2]{0:T(128)}, u32[]{:S(2)}) copy-start(s32[2]{0:T(128)} %add_bitcast_fusion.5) | copy-start | bytes 28
  175.9 4.7 %collective-permute-start.36 = (f32[3,8,128]{2,1,0:T(8,128)S(1)}, f32[3,8,128]{2,1,0:T(8,128)S(1)}, u32[]{:S(2)}, u32[]{:S(2)}) collective-permute-start(f32[3,8,128]{2,1,0:T(8,128)S(1)} %add_select_fusion.8), channel_id=1, source_target_pairs={{8,0},{10,2},{12,4},{14,6},{0,8},{2,10},{4,12},{6,14},{9,1},{11,3}... | collective-permute-start | bytes 36872 | tf_op jit(solution)/shard_map/ppermute | solution.py:16
  180.6 5.6 %collective-permute-start.37 = (f32[3,8,128]{2,1,0:T(8,128)S(1)}, f32[3,8,128]{2,1,0:T(8,128)S(1)}, u32[]{:S(2)}, u32[]{:S(2)}) collective-permute-start(f32[3,8,128]{2,1,0:T(8,128)S(1)} %add.2032), channel_id=1, source_target_pairs={{12,0},{14,2},{0,4},{2,6},{4,8},{6,10},{8,12},{10,14},{13,1},{15,3... | collective-permute-start | bytes 36872 | tf_op jit(solution)/shard_map/ppermute | solution.py:16
  180.8 9.6 %collective-permute-start.29 = (f32[3,16,128]{2,1,0:T(8,128)S(1)}, f32[3,16,128]{2,1,0:T(8,128)S(1)}, u32[]{:S(2)}, u32[]{:S(2)}) collective-permute-start(f32[3,16,128]{2,1,0:T(8,128)S(1)} %fusion.324), channel_id=1, source_target_pairs={{8,0},{10,2},{12,4},{14,6},{0,8},{2,10},{4,12},{6,14},{9,1},{11,3}... | collective-permute-start | bytes 73736 | tf_op jit(solution)/shard_map/ppermute | solution.py:16
  186.2 3.7 %collective-permute-start.38 = (f32[3,8,128]{2,1,0:T(8,128)S(1)}, f32[3,8,128]{2,1,0:T(8,128)S(1)}, u32[]{:S(2)}, u32[]{:S(2)}) collective-permute-start(f32[3,8,128]{2,1,0:T(8,128)S(1)} %add_select_fusion.7), channel_id=1, source_target_pairs={{4,0},{6,2},{8,4},{10,6},{12,8},{14,10},{0,12},{2,14},{5,1},{7,3},... | collective-permute-start | bytes 36872 | tf_op jit(solution)/shard_map/ppermute | solution.py:16
  189.9 6.4 %collective-permute-start.39 = (f32[3,8,128]{2,1,0:T(8,128)S(1)}, f32[3,8,128]{2,1,0:T(8,128)S(1)}, u32[]{:S(2)}, u32[]{:S(2)}) collective-permute-start(f32[3,8,128]{2,1,0:T(8,128)S(1)} %add.2034), channel_id=1, source_target_pairs={{14,0},{0,2},{2,4},{4,6},{6,8},{8,10},{10,12},{12,14},{15,1},{1,3}... | collective-permute-start | bytes 36872 | tf_op jit(solution)/shard_map/ppermute | solution.py:16
  190.5 6.8 %collective-permute-start.30 = (f32[3,16,128]{2,1,0:T(8,128)S(1)}, f32[3,16,128]{2,1,0:T(8,128)S(1)}, u32[]{:S(2)}, u32[]{:S(2)}) collective-permute-start(f32[3,16,128]{2,1,0:T(8,128)S(1)} %add_select_fusion.2), channel_id=1, source_target_pairs={{8,0},{10,2},{12,4},{14,6},{0,8},{2,10},{4,12},{6,14},{9,1},{11,3}... | collective-permute-start | bytes 73736 | tf_op jit(solution)/shard_map/ppermute | solution.py:16
  196.3 3.7 %collective-permute-start.40 = (f32[3,8,128]{2,1,0:T(8,128)S(1)}, f32[3,8,128]{2,1,0:T(8,128)S(1)}, u32[]{:S(2)}, u32[]{:S(2)}) collective-permute-start(f32[3,8,128]{2,1,0:T(8,128)S(1)} %get-tuple-element.569), channel_id=1, source_target_pairs={{2,0},{4,2},{6,4},{8,6},{10,8},{12,10},{14,12},{0,14},{3,1},{5,3},... | collective-permute-start | bytes 36872 | tf_op jit(solution)/shard_map/ppermute | solution.py:16
  197.2 5.7 %collective-permute-start.31 = (f32[3,16,128]{2,1,0:T(8,128)S(1)}, f32[3,16,128]{2,1,0:T(8,128)S(1)}, u32[]{:S(2)}, u32[]{:S(2)}) collective-permute-start(f32[3,16,128]{2,1,0:T(8,128)S(1)} %add.1999), channel_id=1, source_target_pairs={{12,0},{14,2},{0,4},{2,6},{4,8},{6,10},{8,12},{10,14},{13,1},{15,3... | collective-permute-start | bytes 73736 | tf_op jit(solution)/shard_map/ppermute | solution.py:16
  202.9 3.8 %collective-permute-start.32 = (f32[3,16,128]{2,1,0:T(8,128)S(1)}, f32[3,16,128]{2,1,0:T(8,128)S(1)}, u32[]{:S(2)}, u32[]{:S(2)}) collective-permute-start(f32[3,16,128]{2,1,0:T(8,128)S(1)} %add_select_fusion.1), channel_id=1, source_target_pairs={{4,0},{6,2},{8,4},{10,6},{12,8},{14,10},{0,12},{2,14},{5,1},{7,3},... | collective-permute-start | bytes 73736 | tf_op jit(solution)/shard_map/ppermute | solution.py:16
  206.8 6.5 %collective-permute-start.33 = (f32[3,16,128]{2,1,0:T(8,128)S(1)}, f32[3,16,128]{2,1,0:T(8,128)S(1)}, u32[]{:S(2)}, u32[]{:S(2)}) collective-permute-start(f32[3,16,128]{2,1,0:T(8,128)S(1)} %add.2001), channel_id=1, source_target_pairs={{14,0},{0,2},{2,4},{4,6},{6,8},{8,10},{10,12},{12,14},{15,1},{1,3}... | collective-permute-start | bytes 73736 | tf_op jit(solution)/shard_map/ppermute | solution.py:16
  213.3 3.9 %collective-permute-start.34 = (f32[3,16,128]{2,1,0:T(8,128)S(1)}, f32[3,16,128]{2,1,0:T(8,128)S(1)}, u32[]{:S(2)}, u32[]{:S(2)}) collective-permute-start(f32[3,16,128]{2,1,0:T(8,128)S(1)} %get-tuple-element.571), channel_id=1, source_target_pairs={{2,0},{4,2},{6,4},{8,6},{10,8},{12,10},{14,12},{0,14},{3,1},{5,3},... | collective-permute-start | bytes 73736 | tf_op jit(solution)/shard_map/ppermute | solution.py:16
  (15 other events, 71.6 us)
where the time goes:
time: 220 us; the launch traced here: 219 us
  waiting for transfers between devices  68.2 us (31%)
  local copies, waits for them, and re-layouts  57.9 us (26%)
  starting transfers between devices  56.7 us (26%)
  other arithmetic  28.9 us (13%)
  matrix products  4.37 us (2%)
  between operations  2.86 us (1%)
    ppermute x24, waiting for transfers between devices, shifted(): return lax.ppermute(block, axis, route)  53.6 us
    ppermute x8, starting transfers between devices, extended_2(): lax.ppermute(lax.slice_in_dim(block, 0, width, axis=dim), axis, backward)  31.7 us
    ppermute x24, starting transfers between devices, shifted(): return lax.ppermute(block, axis, route)  23 us
    slice x124, local copies, waits for them, and re-layouts, periodic_terms(): forward = jnp.roll(values, -offset, dimension)  19.8 us
    add x28, other arithmetic, hier_axis(): middle = blocks[:, stride] + sense * 0.5 * (left_node + right_node)  12.8 us
    ppermute x8, waiting for transfers between devices, extended_2(): lax.ppermute(lax.slice_in_dim(block, block.shape[dim] - width, None, axis...  10.6 us
    scatter x28, local copies, waits for them, and re-layouts, hier_axis(): blocks = blocks.at[:, stride].set(middle)  10.2 us
    slice x8, local copies, waits for them, and re-layouts, carry_over(): lax.slice_in_dim(result, 0, have_cells, have_cells // common, dimension)  6.52 us
  transfers between devices with their start and end apart: 41, of which 24 were waited for; matrix products, arithmetic and copies ran while one was open for 36% of the time, Pallas kernels for 0%

commit v1 on v0

v1 whole, which is shorter than its diff:
```python
import functools
import math

import jax
import jax.numpy as jnp
import ml_dtypes
import numpy as np
from jax import lax
from jax.experimental import pallas as pl
from jax.experimental.pallas import tpu as pltpu
from jax.sharding import PartitionSpec as P

first_coef = (0.8, -0.2, 4.0 / 105.0, -1.0 / 280.0)
second_coef = (1.6, -0.2, 8.0 / 315.0, -1.0 / 560.0)
second_mid = -205.0 / 72.0
MESH = pl.DeviceIdType.MESH


def hier_matrix(n):
    m = np.eye(n)
    for i in range(1, n):
        s = i & -i
        m[i, i - s] -= 0.5
        m[i, (i + s) % n] -= 0.5
    return m


def tables(za, ya, zb, yb, nx):
    hx, ha, hb = hier_matrix(nx), hier_matrix(ya), hier_matrix(yb)
    dx, da, db = (np.linalg.inv(h) for h in (hx, ha, hb))
    pa, pb = 3 * za, 3 * zb
    ratio = ya // yb
    spread_y = np.zeros((ya, yb))
    spread_y[np.arange(yb) * ratio, np.arange(yb)] = 1
    even = np.zeros((pa, pb))
    swap_a = np.zeros((pa, pa))
    swap_ab = np.zeros((pa, pb))
    swap_b = np.zeros((pb, pb))
    turned = (1, 0, 2)
    for c in range(3):
        for z in range(za):
            even[c * za + z, c * zb + 2 * z] = 1
            swap_a[c * za + z, turned[c] * za + z] = 1
            swap_ab[c * za + z, turned[c] * zb + 2 * z] = 1
        for z in range(zb):
            swap_b[c * zb + z, turned[c] * zb + z] = 1
    own_a = np.concatenate([np.kron(np.eye(pa), ha), np.kron(np.eye(pa), ha[::ratio])])
    own_b = np.concatenate([np.kron(even, spread_y @ hb), np.kron(np.eye(pb), hb)])
    pick_a, pick_b = hx[:: nx // ya], hx[:: nx // yb]
    other_a = np.concatenate([np.tile(pick_a, (pa, 1)), np.tile(pick_b, (pa, 1))])
    other_b = np.concatenate([np.tile(pick_a, (pa, 1)), np.tile(pick_b, (pb, 1))])
    mask_a = np.concatenate([np.kron(swap_a, np.ones((ya, ya))), np.kron(swap_a, np.ones((yb, ya)))])
    mask_b = np.concatenate([np.kron(swap_ab, np.ones((ya, yb))), np.kron(swap_b, np.ones((yb, yb)))])
    spread_a = np.zeros((ya, nx))
    spread_a[np.arange(ya), np.arange(ya) * (nx // ya)] = 1
    spread_b = np.zeros((yb, nx))
    spread_b[np.arange(yb), np.arange(yb) * (nx // yb)] = 1
    place_a = np.tile(ha.T @ spread_a, (pa, 1))
    place_b = np.tile(hb.T @ spread_b, (pb, 1))
    back_a = np.kron(np.eye(pa), da)
    back_b = np.kron(np.eye(pb), db)
    group = (hx.T, dx.T, own_a, own_b, other_a, other_b, mask_a, mask_b, place_a, place_b, back_a, back_b)
    return [np.asarray(m, dtype=ml_dtypes.bfloat16) for m in group]


def terms(x):
    hi = x.astype(jnp.bfloat16)
    lo = (x - hi.astype(jnp.float32)).astype(jnp.bfloat16)
    return hi, lo


def dot(a, b, contract):
    return lax.dot_general(a, b, (contract, ((), ())), preferred_element_type=jnp.float32)


def right(x, m):
    return sum(dot(t, m, ((1,), (0,))) for t in terms(x))


def left(m, x):
    return sum(dot(m, t, ((1,), (0,))) for t in terms(x))


def left_t(m, x):
    return sum(dot(m, t, ((1,), (1,))) for t in terms(x))


def body(n, step, viscosity, space_a, space_b, *refs):
    (coeffs, a_ref, b_ref, hx, dx, own_a, own_b, other_a, other_b, mask_a, mask_b,
     place_a, place_b, back_a, back_b,
     out_a, out_b, comb_a, comb_b,
     pad_a, pad_b, adv_a, adv_b, got_a, got_b, head, nxt, low, high, nodal,
     send_sem, recv_sem, swap_send, swap_recv, head_send, head_recv) = refs
    za, ya, nx = a_ref.shape[2:]
    zb, yb = b_ref.shape[2:4]
    rows = 3 * za * ya
    me = lax.axis_index("slab")
    member = lax.axis_index("grid")
    partner = 1 - member
    ahead, behind = lax.rem(me + 1, n), lax.rem(me + n - 1, n)

    distances = [2**e for e in range(n.bit_length() - 1)]
    offsets = sorted({o % n for d in distances for o in (d, n - d)})
    barrier = pltpu.get_barrier_semaphore()
    for o in offsets:
        pl.semaphore_signal(barrier, inc=1, device_id={"slab": lax.rem(me + o, n)}, device_id_type=MESH)
    pl.semaphore_signal(barrier, inc=1, device_id={"grid": partner}, device_id_type=MESH)
    pad_a[0, :, 4 : 4 + za] = a_ref[0]
    pad_b[0, :, 4 : 4 + zb] = b_ref[0]
    pl.semaphore_wait(barrier, len(offsets) + 1)

    def halo(pad, depth, stage, which):
        made = []
        for side, (first, target, peer) in enumerate(((depth, 0, ahead), (4, 4 + depth, behind))):
            made.append(pltpu.make_async_remote_copy(
                src_ref=pad.at[stage, :, pl.ds(first, 4)],
                dst_ref=pad.at[stage, :, pl.ds(target, 4)],
                send_sem=send_sem.at[stage, which, side],
                recv_sem=recv_sem.at[stage, which, side],
                device_id={"slab": peer}, device_id_type=MESH))
        for copy in made:
            copy.start()
        return made

    def flat_rate(f, spaces):
        planes, y, x = f.shape[1:]
        rows_f = f.reshape(3 * planes * y, x)
        blocks = f.reshape(3 * planes, y, x)
        mid = second_mid * viscosity * sum(1.0 / (h * h) for h in spaces)

        def direction(value, axis, h):
            grad = curv = None
            length = value.shape[axis]
            for k in range(1, 5):
                fwd = pltpu.roll(value, length - k, axis)
                bwd = pltpu.roll(value, k, axis)
                g = (first_coef[k - 1] / h) * (fwd - bwd)
                c = (viscosity * second_coef[k - 1] / (h * h)) * (fwd + bwd)
                grad = g if grad is None else grad + g
                curv = c if curv is None else curv + c
            return grad.reshape(f.shape), curv.reshape(f.shape)

        xg, xc = direction(rows_f, 1, spaces[2])
        yg, yc = direction(blocks, 1, spaces[1])
        return mid * f + xc + yc - (f[0:1] * xg + f[1:2] * yg)

    def z_rate(pad, stage, depth, h):
        f = pad[stage, :, 4 : 4 + depth]
        grad = curv = None
        for k in range(1, 5):
            fwd = pad[stage, :, 4 + k : 4 + k + depth]
            bwd = pad[stage, :, 4 - k : 4 - k + depth]
            g = (first_coef[k - 1] / h) * (fwd - bwd)
            c = (viscosity * second_coef[k - 1] / (h * h)) * (fwd + bwd)
            grad = g if grad is None else grad + g
            curv = c if curv is None else curv + c
        return curv - f[2:3] * grad

    grids = ((pad_a, za, space_a, adv_a), (pad_b, zb, space_b, adv_b))
    swaps = []
    flights = [halo(pad, depth, 0, w) for w, (pad, depth, _, _) in enumerate(grids)]
    sent = list(flights)
    for stage in range(4):
        flat = [flat_rate(pad[stage, :, 4 : 4 + depth], spaces) for pad, depth, spaces, _ in grids]
        coming = []
        for w, (pad, depth, spaces, adv) in enumerate(grids):
            for copy in flights[w]:
                copy.wait_recv()
            k = flat[w] + z_rate(pad, stage, depth, spaces[0])
            base = pad[0, :, 4 : 4 + depth]
            share = step / 6.0 * (1.0, 2.0, 2.0, 1.0)[stage]
            adv[...] = (base if stage == 0 else adv[...]) + share * k
            if stage < 3:
                pad[stage + 1, :, 4 : 4 + depth] = base + (0.5, 0.5, 1.0)[stage] * step * k
                coming.append(halo(pad, depth, stage + 1, w))
            else:
                copy = pltpu.make_async_remote_copy(
                    src_ref=adv, dst_ref=(got_a, got_b)[w],
                    send_sem=swap_send.at[w], recv_sem=swap_recv.at[w],
                    device_id={"grid": partner}, device_id_type=MESH)
                copy.start()
                swaps.append(copy)
        if stage < 3:
            flights = coming
            sent.extend(coming)

    weight = [coeffs[i].astype(jnp.float32) for i in (member, partner, 2 + member, 2 + partner)]
    mine_a = weight[0] * left(own_a[...], right(adv_a[...].reshape(rows, nx), hx[...]))
    mine_b = weight[2] * left(own_b[...], right(adv_b[...].reshape(rows, nx), hx[...]))

    def other(got, pick, mask, place):
        crossed = left_t(pick[...], got[...].reshape(rows, nx)) * mask[...].astype(jnp.float32)
        return right(crossed, place[...])

    swaps[0].wait_recv()
    sum_a = mine_a + weight[1] * other(got_a, other_a, mask_a, place_a)
    swaps[1].wait_recv()
    sum_b = mine_b + weight[3] * other(got_b, other_b, mask_b, place_b)
    nodal_a = sum_a[:rows] + sum_b[:rows]
    level_a = nodal_a.reshape(3, za, ya, nx)
    part_q = sum_a[rows:].reshape(3, za, yb, nx)
    part_p = sum_b[rows:].reshape(3, zb, yb, nx)

    head[:, 0:ya] = level_a[:, 0]
    head[:, ya : ya + yb] = part_p[:, 0]
    head[:, ya + yb : ya + 2 * yb] = part_q[:, 0]

    @pl.when(me == 0)
    def _():
        low[...] = jnp.zeros_like(low)
        high[...] = jnp.zeros_like(high)

    def head_copy(target, peer, send, recv):
        return pltpu.make_async_remote_copy(
            src_ref=head, dst_ref=target, send_sem=head_send.at[send], recv_sem=head_recv.at[recv],
            device_id={"slab": peer}, device_id_type=MESH)

    to_behind = head_copy(nxt, behind, 0, 0)
    to_behind.start()
    for e, d in enumerate(distances):
        @pl.when(lax.rem(me, 2 * d) == 0)
        def _(e=e, d=d):
            head_copy(low, lax.rem(me + d, n), 1 + 2 * e, 1).start()
            head_copy(high, lax.rem(me + n - d, n), 2 + 2 * e, 2).start()

    out_a[0] = left(back_a[...], right(nodal_a, dx[...])).reshape(3, za, ya, nx)

    to_behind.wait_recv()
    next_a = nxt[:, 0:ya]
    next_p = nxt[:, ya : ya + yb]
    next_q = nxt[:, ya + yb : ya + 2 * yb]
    for z in range(za):
        q_now = part_q[:, z]
        q_next = part_q[:, z + 1] if z + 1 < za else next_q
        p_next = part_p[:, 2 * z + 2] if z + 1 < za else next_p
        nodal[:, 2 * z] = part_p[:, 2 * z] + q_now
        nodal[:, 2 * z + 1] = part_p[:, 2 * z + 1] + 0.5 * (q_now + q_next)
        comb_b[0, :, 2 * z + 1] = part_p[:, 2 * z + 1] - 0.5 * (part_p[:, 2 * z] + p_next)
    out_b[0] = left(back_b[...], right(nodal[...].reshape(rows, nx), dx[...])).reshape(3, zb, yb, nx)

    even_b = [part_p[:, 2 * z] + part_q[:, z] for z in range(za)] + [next_p + next_q]
    even_a = [level_a[:, z] for z in range(za)] + [next_a]
    for z in range(1, za):
        s = z & -z
        comb_a[0, :, z] = even_a[z] - 0.5 * (even_a[z - s] + even_a[z + s])
        comb_b[0, :, 2 * z] = even_b[z] - 0.5 * (even_b[z - s] + even_b[z + s])

    @pl.when(me != 0)
    def _():
        head_copy(low, behind, 0, 1).wait_recv()
        head_copy(high, behind, 0, 2).wait_recv()

    ends = low[...] + high[...]
    comb_a[0, :, 0] = even_a[0] - 0.5 * ends[:, 0:ya]
    comb_b[0, :, 0] = even_b[0] - 0.5 * (ends[:, ya : ya + yb] + ends[:, ya + yb : ya + 2 * yb])

    for pair in sent:
        for copy in pair:
            copy.wait_send()
    for copy in swaps:
        copy.wait_send()
    to_behind.wait_send()
    for e, d in enumerate(distances):
        @pl.when(lax.rem(me, 2 * d) == 0)
        def _(e=e, d=d):
            head_copy(low, behind, 1 + 2 * e, 1).wait_send()
            head_copy(high, behind, 2 + 2 * e, 2).wait_send()


def shards(n, grids_a, grids_b, coeffs):
    za, ya, nx = grids_a.shape[2:]
    zb, yb = grids_b.shape[2:4]
    finest = 2.0 * math.pi / max(nx, 2 * za * n)
    step, viscosity = 0.1 * finest, 0.2 * finest
    space_a = (2.0 * math.pi / (za * n), 2.0 * math.pi / ya, 2.0 * math.pi / nx)
    space_b = (2.0 * math.pi / (zb * n), 2.0 * math.pi / yb, 2.0 * math.pi / nx)
    consts = [jnp.asarray(m) for m in tables(za, ya, zb, yb, nx)]
    exponents = n.bit_length() - 1
    f32 = jnp.float32
    head_shape = (3, ya + 2 * yb, nx)
    vmem = pl.BlockSpec(memory_space=pltpu.VMEM)
    shape_a = jax.ShapeDtypeStruct(grids_a.shape, f32)
    shape_b = jax.ShapeDtypeStruct(grids_b.shape, f32)
    return pl.pallas_call(
        functools.partial(body, n, step, viscosity, space_a, space_b),
        out_shape=(shape_a, shape_b, shape_a, shape_b),
        in_specs=[pl.BlockSpec(memory_space=pltpu.SMEM)] + [vmem] * (2 + len(consts)),
        out_specs=(vmem,) * 4,
        scratch_shapes=[
            pltpu.VMEM((4, 3, za + 8, ya, nx), f32),
            pltpu.VMEM((4, 3, zb + 8, yb, nx), f32),
            pltpu.VMEM((3, za, ya, nx), f32),
            pltpu.VMEM((3, zb, yb, nx), f32),
            pltpu.VMEM((3, za, ya, nx), f32),
            pltpu.VMEM((3, zb, yb, nx), f32),
            pltpu.VMEM(head_shape, f32),
            pltpu.VMEM(head_shape, f32),
            pltpu.VMEM(head_shape, f32),
            pltpu.VMEM(head_shape, f32),
            pltpu.VMEM((3, zb, yb, nx), f32),
            pltpu.SemaphoreType.DMA((4, 2, 2)),
            pltpu.SemaphoreType.DMA((4, 2, 2)),
            pltpu.SemaphoreType.DMA((2,)),
            pltpu.SemaphoreType.DMA((2,)),
            pltpu.SemaphoreType.DMA((1 + 2 * exponents,)),
            pltpu.SemaphoreType.DMA((3,)),
        ],
        compiler_params=pltpu.CompilerParams(
            collective_id=0, has_side_effects=True, vmem_limit_bytes=32 * 2**20),
    )(coeffs, grids_a, grids_b, *consts)


def solution(mesh):
    split = P(("groups", "grid"), None, "slab", None, None)
    return jax.shard_map(
        functools.partial(shards, mesh.shape["slab"]),
        mesh=mesh,
        in_specs=(split, split, P()),
        out_specs=(split, split, split, split),
        check_vma=False,
    )
```

time: 220 us -> 60 us (0.27)
  waiting for transfers between devices: 68.2 us -> 0 us
  starting transfers between devices: 56.7 us -> 0 us
  Pallas kernels: 0 us -> 43.3 us
  local copies, waits for them, and re-layouts: 57.9 us -> 15.3 us
  other arithmetic: 28.9 us -> 0 us
  matrix products: 4.37 us -> 0 us
    ppermute x41 -> x0, waiting for transfers between devices: 68.2 us -> none  [the longest x24 53.6 us: shifted(): return lax.ppermute(block, axis, route)]
    ppermute x41 -> x0, starting transfers between devices: 56.7 us -> none  [the longest x8 31.7 us: extended_2(): lax.ppermute(lax.slice_in_dim(block, 0, width, axis=dim), axis, backward)]
    pallas_call x0 -> x1, Pallas kernels: none -> 43.3 us  [shards(): pl.pallas_call(functools.partial(body, n, step, viscosity, space_a, space...]
    slice x183 -> x0, local copies, waits for them, and re-layouts: 35 us -> none  [the longest x124 19.8 us: periodic_terms(): forward = jnp.roll(values, -offset, dimension)]
    add x59 -> x0, other arithmetic: 23.8 us -> none  [the longest x28 12.8 us: hier_axis(): middle = blocks[:, stride] + sense * 0.5 * (left_node + right_node)]
    scatter x38 -> x0, local copies, waits for them, and re-layouts: 14.2 us -> none  [the longest x28 10.2 us: hier_axis(): blocks = blocks.at[:, stride].set(middle)]
    unnamed x50 -> x34, local copies, waits for them, and re-layouts: 1.65 us -> 15.3 us
    mul x13 -> x0, other arithmetic: 4.65 us -> none  [the longest x5 3.3 us: gather_terms(): term = weight * carry_over(source, target_dims)]
  transfers between devices with their start and end apart: 41 -> 0, of which waited for: 24 -> 0; matrix products, arithmetic and copies ran while one was open for 36% -> 0% of each run, Pallas kernels for 0% -> 0%
where the time goes in v1:
time: 60 us; the launch traced here: 59.3 us
  Pallas kernels  43.3 us (72%)
  local copies, waits for them, and re-layouts  15.3 us (26%)
  between operations  0.66 us (1%)
    pallas_call x1, Pallas kernels, shards(): pl.pallas_call(functools.partial(body, n, step, viscosity, space_a, space...  43.3 us
    unnamed x34, local copies, waits for them, and re-layouts  15.3 us

profile of v1, /device:TPU:0, one launch (start us, length us, event | category | flops | bytes accessed | tf_op | source)
XLA Modules:
  0.0 59.3 jit_solution(5982172501003851936)
XLA Ops:
  0.6 0.0 copy-start
  0.6 0.9 %copy-done = bf16[384,192]{1,0:T(8,128)(2,1)S(1)} copy-done((bf16[384,192]{1,0:T(8,128)(2,1)S(1)}, bf16[384,192]{1,0:T(8,128)(2,1)}, u32[]{:S(2)}) %copy-start) | copy-done | bytes 147480
  1.6 0.0 copy-start.1
  1.6 0.9 %copy-done.1 = bf16[384,192]{1,0:T(8,128)(2,1)S(1)} copy-done((bf16[384,192]{1,0:T(8,128)(2,1)S(1)}, bf16[384,192]{1,0:T(8,128)(2,1)}, u32[]{:S(2)}) %copy-start.1) | copy-done | bytes 147480
  2.5 0.0 copy-start.2
  2.5 0.9 %copy-done.2 = bf16[288,192]{1,0:T(8,128)(2,1)S(1)} copy-done((bf16[288,192]{1,0:T(8,128)(2,1)S(1)}, bf16[288,192]{1,0:T(8,128)(2,1)}, u32[]{:S(2)}) %copy-start.2) | copy-done | bytes 110616
  3.4 0.0 copy-start.3
  3.4 0.9 %copy-done.3 = bf16[288,192]{1,0:T(8,128)(2,1)S(1)} copy-done((bf16[288,192]{1,0:T(8,128)(2,1)S(1)}, bf16[288,192]{1,0:T(8,128)(2,1)}, u32[]{:S(2)}) %copy-start.3) | copy-done | bytes 110616
  4.3 0.0 copy-start.4
  4.3 0.9 %copy-done.4 = f32[1,3,4,16,128]{4,3,2,1,0:T(8,128)S(1)} copy-done((f32[1,3,4,16,128]{4,3,2,1,0:T(8,128)S(1)}, f32[1,3,4,16,128]{4,3,2,1,0:T(8,128)}, u32[]{:S(2)}) %copy-start.4) | copy-done | bytes 98328
  5.2 0.0 copy-start.5
  5.2 0.9 %copy-done.5 = f32[1,3,8,8,128]{4,3,2,1,0:T(8,128)S(1)} copy-done((f32[1,3,8,8,128]{4,3,2,1,0:T(8,128)S(1)}, f32[1,3,8,8,128]{4,3,2,1,0:T(8,128)}, u32[]{:S(2)}) %copy-start.5) | copy-done | bytes 98328
  6.1 0.0 copy-start.6
  6.1 0.9 %copy-done.6 = bf16[192,192]{1,0:T(8,128)(2,1)S(1)} copy-done((bf16[192,192]{1,0:T(8,128)(2,1)S(1)}, bf16[192,192]{1,0:T(8,128)(2,1)}, u32[]{:S(2)}) %copy-start.6) | copy-done | bytes 73752
  7.0 0.0 copy-start.7
  7.0 0.9 %copy-done.7 = bf16[192,192]{1,0:T(8,128)(2,1)S(1)} copy-done((bf16[192,192]{1,0:T(8,128)(2,1)S(1)}, bf16[192,192]{1,0:T(8,128)(2,1)}, u32[]{:S(2)}) %copy-start.7) | copy-done | bytes 73752
  7.9 0.0 copy-start.8
  7.9 0.9 %copy-done.8 = bf16[384,128]{1,0:T(8,128)(2,1)S(1)} copy-done((bf16[384,128]{1,0:T(8,128)(2,1)S(1)}, bf16[384,128]{1,0:T(8,128)(2,1)}, u32[]{:S(2)}) %copy-start.8) | copy-done | bytes 98328
  8.8 0.0 copy-start.9
  8.8 0.9 %copy-done.9 = bf16[288,128]{1,0:T(8,128)(2,1)S(1)} copy-done((bf16[288,128]{1,0:T(8,128)(2,1)S(1)}, bf16[288,128]{1,0:T(8,128)(2,1)}, u32[]{:S(2)}) %copy-start.9) | copy-done | bytes 73752
  9.7 0.0 copy-start.10
  9.7 0.8 %copy-done.10 = bf16[192,128]{1,0:T(8,128)(2,1)S(1)} copy-done((bf16[192,128]{1,0:T(8,128)(2,1)S(1)}, bf16[192,128]{1,0:T(8,128)(2,1)}, u32[]{:S(2)}) %copy-start.10) | copy-done | bytes 49176
  10.5 0.0 copy-start.11
  10.5 0.8 %copy-done.11 = bf16[192,128]{1,0:T(8,128)(2,1)S(1)} copy-done((bf16[192,128]{1,0:T(8,128)(2,1)S(1)}, bf16[192,128]{1,0:T(8,128)(2,1)}, u32[]{:S(2)}) %copy-start.11) | copy-done | bytes 49176
  11.3 0.0 copy-start.12
  11.3 0.8 %copy-done.12 = bf16[128,128]{1,0:T(8,128)(2,1)S(1)} copy-done((bf16[128,128]{1,0:T(8,128)(2,1)S(1)}, bf16[128,128]{1,0:T(8,128)(2,1)}, u32[]{:S(2)}) %copy-start.12) | copy-done | bytes 32792
  12.0 0.0 copy-start.13
  12.0 0.8 %copy-done.13 = bf16[128,128]{1,0:T(8,128)(2,1)S(1)} copy-done((bf16[128,128]{1,0:T(8,128)(2,1)S(1)}, bf16[128,128]{1,0:T(8,128)(2,1)}, u32[]{:S(2)}) %copy-start.13) | copy-done | bytes 32792
  12.8 0.0 copy-start.14
  12.8 0.7 %copy-done.14 = s32[4]{0:T(128)S(1)} copy-done((s32[4]{0:T(128)S(1)}, s32[4]{0:T(128)}, u32[]{:S(2)}) %copy-start.14) | copy-done | bytes 40
  13.4 43.3 %shard_map.174 = (f32[1,3,4,16,128]{4,3,2,1,0:T(8,128)S(1)}, f32[1,3,8,8,128]{4,3,2,1,0:T(8,128)S(1)}, f32[1,3,4,16,128]{4,3,2,1,0:T(8,128)S(1)}, f32[1,3,8,8,128]{4,3,2,1,0:T(8,128)S(1)}) custom-call(s32[4]{0:T(128)S(1)} %copy-done.14, f32[1,3,4,16,128]{4,3,2,1,0:T(8,128)S(1)} %copy-done.4, f32[1,3,8,8,128]{4,3,2,1,0:T(8,128)S(1)} %copy-done.5, ...), custom_call_target="tpu_custom_call" | custom-call | tf_op jit(solution)/shard_map/pallas_call | solution.py:284
  56.8 0.6 %copy.23 = f32[1,3,4,16,128]{4,3,2,1,0:T(8,128)} copy(f32[1,3,4,16,128]{4,3,2,1,0:T(8,128)S(1)} %get-tuple-element.8) | data formatting | bytes 196608
  57.4 0.6 %copy.24 = f32[1,3,8,8,128]{4,3,2,1,0:T(8,128)} copy(f32[1,3,8,8,128]{4,3,2,1,0:T(8,128)S(1)} %get-tuple-element.9) | data formatting | bytes 196608
  58.1 0.6 %copy.25 = f32[1,3,4,16,128]{4,3,2,1,0:T(8,128)} copy(f32[1,3,4,16,128]{4,3,2,1,0:T(8,128)S(1)} %get-tuple-element.10) | data formatting | bytes 196608
  58.7 0.6 %copy.26 = f32[1,3,8,8,128]{4,3,2,1,0:T(8,128)} copy(f32[1,3,8,8,128]{4,3,2,1,0:T(8,128)S(1)} %get-tuple-element.11) | data formatting | bytes 196608
Async XLA Ops:
  0.6 0.9 %copy-start = (bf16[384,192]{1,0:T(8,128)(2,1)S(1)}, bf16[384,192]{1,0:T(8,128)(2,1)}, u32[]{:S(2)}) copy-start(bf16[384,192]{1,0:T(8,128)(2,1)} %constant.31.clone.refs_10_) | copy-start | bytes 442372
  1.6 0.9 %copy-start.1 = (bf16[384,192]{1,0:T(8,128)(2,1)S(1)}, bf16[384,192]{1,0:T(8,128)(2,1)}, u32[]{:S(2)}) copy-start(bf16[384,192]{1,0:T(8,128)(2,1)} %constant.27.clone.refs_6_) | copy-start | bytes 442372
  2.5 0.9 %copy-start.2 = (bf16[288,192]{1,0:T(8,128)(2,1)S(1)}, bf16[288,192]{1,0:T(8,128)(2,1)}, u32[]{:S(2)}) copy-start(bf16[288,192]{1,0:T(8,128)(2,1)} %constant.30.clone.refs_9_) | copy-start | bytes 331780
  3.4 0.9 %copy-start.3 = (bf16[288,192]{1,0:T(8,128)(2,1)S(1)}, bf16[288,192]{1,0:T(8,128)(2,1)}, u32[]{:S(2)}) copy-start(bf16[288,192]{1,0:T(8,128)(2,1)} %constant.26.clone.refs_5_) | copy-start | bytes 331780
  4.3 0.9 %copy-start.4 = (f32[1,3,4,16,128]{4,3,2,1,0:T(8,128)S(1)}, f32[1,3,4,16,128]{4,3,2,1,0:T(8,128)}, u32[]{:S(2)}) copy-start(f32[1,3,4,16,128]{4,3,2,1,0:T(8,128)} %refs_1_.1) | copy-start | bytes 294916
  5.2 0.9 %copy-start.5 = (f32[1,3,8,8,128]{4,3,2,1,0:T(8,128)S(1)}, f32[1,3,8,8,128]{4,3,2,1,0:T(8,128)}, u32[]{:S(2)}) copy-start(f32[1,3,8,8,128]{4,3,2,1,0:T(8,128)} %refs_2_.1) | copy-start | bytes 294916
  6.1 0.9 %copy-start.6 = (bf16[192,192]{1,0:T(8,128)(2,1)S(1)}, bf16[192,192]{1,0:T(8,128)(2,1)}, u32[]{:S(2)}) copy-start(bf16[192,192]{1,0:T(8,128)(2,1)} %constant.35.clone.refs_14_) | copy-start | bytes 221188
  7.0 0.9 %copy-start.7 = (bf16[192,192]{1,0:T(8,128)(2,1)S(1)}, bf16[192,192]{1,0:T(8,128)(2,1)}, u32[]{:S(2)}) copy-start(bf16[192,192]{1,0:T(8,128)(2,1)} %constant.34.clone.refs_13_) | copy-start | bytes 221188
  7.9 0.9 %copy-start.8 = (bf16[384,128]{1,0:T(8,128)(2,1)S(1)}, bf16[384,128]{1,0:T(8,128)(2,1)}, u32[]{:S(2)}) copy-start(bf16[384,128]{1,0:T(8,128)(2,1)} %constant.29.clone.refs_8_) | copy-start | bytes 294916
  8.8 0.9 %copy-start.9 = (bf16[288,128]{1,0:T(8,128)(2,1)S(1)}, bf16[288,128]{1,0:T(8,128)(2,1)}, u32[]{:S(2)}) copy-start(bf16[288,128]{1,0:T(8,128)(2,1)} %constant.28.clone.refs_7_) | copy-start | bytes 221188
  9.7 0.8 %copy-start.10 = (bf16[192,128]{1,0:T(8,128)(2,1)S(1)}, bf16[192,128]{1,0:T(8,128)(2,1)}, u32[]{:S(2)}) copy-start(bf16[192,128]{1,0:T(8,128)(2,1)} %constant.33.clone.refs_12_) | copy-start | bytes 147460
  10.5 0.8 %copy-start.11 = (bf16[192,128]{1,0:T(8,128)(2,1)S(1)}, bf16[192,128]{1,0:T(8,128)(2,1)}, u32[]{:S(2)}) copy-start(bf16[192,128]{1,0:T(8,128)(2,1)} %constant.32.clone.refs_11_) | copy-start | bytes 147460
  11.3 0.8 %copy-start.12 = (bf16[128,128]{1,0:T(8,128)(2,1)S(1)}, bf16[128,128]{1,0:T(8,128)(2,1)}, u32[]{:S(2)}) copy-start(bf16[128,128]{1,0:T(8,128)(2,1)} %constant.25.clone.refs_4_) | copy-start | bytes 98308
  12.0 0.8 %copy-start.13 = (bf16[128,128]{1,0:T(8,128)(2,1)S(1)}, bf16[128,128]{1,0:T(8,128)(2,1)}, u32[]{:S(2)}) copy-start(bf16[128,128]{1,0:T(8,128)(2,1)} %constant.24.clone.refs_3_) | copy-start | bytes 98308
  12.8 0.7 %copy-start.14 = (s32[4]{0:T(128)S(1)}, s32[4]{0:T(128)}, u32[]{:S(2)}) copy-start(s32[4]{0:T(128)} %refs_0_.1) | copy-start | bytes 52

commit v2 on v1

--- a/solution.py
+++ b/solution.py
@@ -86,11 +86,16 @@
 
 
 def body(n, step, viscosity, space_a, space_b, *refs):
-    (coeffs, a_ref, b_ref, hx, dx, own_a, own_b, other_a, other_b, mask_a, mask_b,
-     place_a, place_b, back_a, back_b,
-     out_a, out_b, comb_a, comb_b,
-     pad_a, pad_b, adv_a, adv_b, got_a, got_b, head, nxt, low, high, nodal,
-     send_sem, recv_sem, swap_send, swap_recv, head_send, head_recv) = refs
+    count = 12
+    coeffs, a_ref, b_ref = refs[:3]
+    tables_far = refs[3 : 3 + count]
+    results = refs[3 + count : 7 + count]
+    tables_near = refs[7 + count : 7 + 2 * count]
+    (hx, dx, own_a, own_b, other_a, other_b, mask_a, mask_b,
+     place_a, place_b, back_a, back_b) = tables_near
+    (out_a, out_b, comb_a, comb_b, pad_a, pad_b, adv_a, adv_b, got_a, got_b, head, nxt, low, high, nodal,
+     send_sem, recv_sem, swap_send, swap_recv, head_send, head_recv,
+     in_sem, table_sem, out_sem) = refs[7 + 2 * count :]
     za, ya, nx = a_ref.shape[2:]
     zb, yb = b_ref.shape[2:4]
     rows = 3 * za * ya
@@ -105,8 +110,22 @@
     for o in offsets:
         pl.semaphore_signal(barrier, inc=1, device_id={"slab": lax.rem(me + o, n)}, device_id_type=MESH)
     pl.semaphore_signal(barrier, inc=1, device_id={"grid": partner}, device_id_type=MESH)
-    pad_a[0, :, 4 : 4 + za] = a_ref[0]
-    pad_b[0, :, 4 : 4 + zb] = b_ref[0]
+    loads = [
+        pltpu.make_async_copy(a_ref.at[0], pad_a.at[0, :, pl.ds(4, za)], in_sem.at[0]),
+        pltpu.make_async_copy(b_ref.at[0], pad_b.at[0, :, pl.ds(4, zb)], in_sem.at[1]),
+    ]
+    fetches = [
+        pltpu.make_async_copy(far, near, table_sem.at[i])
+        for i, (far, near) in enumerate(zip(tables_far, tables_near))
+    ]
+    for copy in loads + fetches:
+        copy.start()
+    stores = [
+        pltpu.make_async_copy(near, far.at[0], out_sem.at[i])
+        for i, (near, far) in enumerate(zip((out_a, out_b, comb_a, comb_b), results))
+    ]
+    for copy in loads:
+        copy.wait()
     pl.semaphore_wait(barrier, len(offsets) + 1)
 
     def halo(pad, depth, stage, which):
@@ -184,6 +203,8 @@
             flights = coming
             sent.extend(coming)
 
+    for copy in fetches:
+        copy.wait()
     weight = [coeffs[i].astype(jnp.float32) for i in (member, partner, 2 + member, 2 + partner)]
     mine_a = weight[0] * left(own_a[...], right(adv_a[...].reshape(rows, nx), hx[...]))
     mine_b = weight[2] * left(own_b[...], right(adv_b[...].reshape(rows, nx), hx[...]))
@@ -201,18 +222,22 @@
     part_q = sum_a[rows:].reshape(3, za, yb, nx)
     part_p = sum_b[rows:].reshape(3, zb, yb, nx)
 
+    coarse = head.at[:, pl.ds(0, ya + yb)]
     head[:, 0:ya] = level_a[:, 0]
-    head[:, ya : ya + yb] = part_p[:, 0]
+    head[:, ya : ya + yb] = part_p[:, 0] + part_q[:, 0]
     head[:, ya + yb : ya + 2 * yb] = part_q[:, 0]
 
     @pl.when(me == 0)
     def _():
         low[...] = jnp.zeros_like(low)
+
+    @pl.when(me == 0)
+    def _():
         high[...] = jnp.zeros_like(high)
 
     def head_copy(target, peer, send, recv):
         return pltpu.make_async_remote_copy(
-            src_ref=head, dst_ref=target, send_sem=head_send.at[send], recv_sem=head_recv.at[recv],
+            src_ref=head if recv == 0 else coarse, dst_ref=target, send_sem=head_send.at[send], recv_sem=head_recv.at[recv],
             device_id={"slab": peer}, device_id_type=MESH)
 
     to_behind = head_copy(nxt, behind, 0, 0)
@@ -221,38 +246,55 @@
         @pl.when(lax.rem(me, 2 * d) == 0)
         def _(e=e, d=d):
             head_copy(low, lax.rem(me + d, n), 1 + 2 * e, 1).start()
-            head_copy(high, lax.rem(me + n - d, n), 2 + 2 * e, 2).start()
-
-    out_a[0] = left(back_a[...], right(nodal_a, dx[...])).reshape(3, za, ya, nx)
+            if 1 < d < n // 2:
+                head_copy(high, lax.rem(me + n - d, n), 2 + 2 * e, 2).start()
+
+    out_a[...] = left(back_a[...], right(nodal_a, dx[...])).reshape(3, za, ya, nx)
+    stores[0].start()
 
     to_behind.wait_recv()
     next_a = nxt[:, 0:ya]
-    next_p = nxt[:, ya : ya + yb]
+    next_b = nxt[:, ya : ya + yb]
     next_q = nxt[:, ya + yb : ya + 2 * yb]
+    next_p = next_b - next_q
     for z in range(za):
         q_now = part_q[:, z]
         q_next = part_q[:, z + 1] if z + 1 < za else next_q
         p_next = part_p[:, 2 * z + 2] if z + 1 < za else next_p
         nodal[:, 2 * z] = part_p[:, 2 * z] + q_now
         nodal[:, 2 * z + 1] = part_p[:, 2 * z + 1] + 0.5 * (q_now + q_next)
-        comb_b[0, :, 2 * z + 1] = part_p[:, 2 * z + 1] - 0.5 * (part_p[:, 2 * z] + p_next)
-    out_b[0] = left(back_b[...], right(nodal[...].reshape(rows, nx), dx[...])).reshape(3, zb, yb, nx)
-
-    even_b = [part_p[:, 2 * z] + part_q[:, z] for z in range(za)] + [next_p + next_q]
+        comb_b[:, 2 * z + 1] = part_p[:, 2 * z + 1] - 0.5 * (part_p[:, 2 * z] + p_next)
+    out_b[...] = left(back_b[...], right(nodal[...].reshape(rows, nx), dx[...])).reshape(3, zb, yb, nx)
+    stores[1].start()
+
+    even_b = [part_p[:, 2 * z] + part_q[:, z] for z in range(za)] + [next_b]
     even_a = [level_a[:, z] for z in range(za)] + [next_a]
     for z in range(1, za):
         s = z & -z
-        comb_a[0, :, z] = even_a[z] - 0.5 * (even_a[z - s] + even_a[z + s])
-        comb_b[0, :, 2 * z] = even_b[z] - 0.5 * (even_b[z - s] + even_b[z + s])
+        comb_a[:, z] = even_a[z] - 0.5 * (even_a[z - s] + even_a[z + s])
+        comb_b[:, 2 * z] = even_b[z] - 0.5 * (even_b[z - s] + even_b[z + s])
 
     @pl.when(me != 0)
     def _():
         head_copy(low, behind, 0, 1).wait_recv()
+
+    @pl.when((me != 0) & (lax.rem(me, 2) == 0) & (me != n // 2))
+    def _():
         head_copy(high, behind, 0, 2).wait_recv()
 
+    @pl.when(lax.rem(me, 2) == 1)
+    def _():
+        high[...] = nxt[:, 0 : ya + yb]
+
+    @pl.when(me == n // 2)
+    def _():
+        high[...] = low[...]
+
     ends = low[...] + high[...]
-    comb_a[0, :, 0] = even_a[0] - 0.5 * ends[:, 0:ya]
-    comb_b[0, :, 0] = even_b[0] - 0.5 * (ends[:, ya : ya + yb] + ends[:, ya + yb : ya + 2 * yb])
+    comb_a[:, 0] = even_a[0] - 0.5 * ends[:, 0:ya]
+    comb_b[:, 0] = even_b[0] - 0.5 * ends[:, ya : ya + yb]
+    stores[2].start()
+    stores[3].start()
 
     for pair in sent:
         for copy in pair:
@@ -264,7 +306,10 @@
         @pl.when(lax.rem(me, 2 * d) == 0)
         def _(e=e, d=d):
             head_copy(low, behind, 1 + 2 * e, 1).wait_send()
-            head_copy(high, behind, 2 + 2 * e, 2).wait_send()
+            if 1 < d < n // 2:
+                head_copy(high, behind, 2 + 2 * e, 2).wait_send()
+    for copy in stores:
+        copy.wait()
 
 
 def shards(n, grids_a, grids_b, coeffs):
@@ -278,15 +323,20 @@
     exponents = n.bit_length() - 1
     f32 = jnp.float32
     head_shape = (3, ya + 2 * yb, nx)
-    vmem = pl.BlockSpec(memory_space=pltpu.VMEM)
+    coarse_shape = (3, ya + yb, nx)
+    far = pl.BlockSpec(memory_space=pltpu.HBM)
     shape_a = jax.ShapeDtypeStruct(grids_a.shape, f32)
     shape_b = jax.ShapeDtypeStruct(grids_b.shape, f32)
     return pl.pallas_call(
         functools.partial(body, n, step, viscosity, space_a, space_b),
         out_shape=(shape_a, shape_b, shape_a, shape_b),
-        in_specs=[pl.BlockSpec(memory_space=pltpu.SMEM)] + [vmem] * (2 + len(consts)),
-        out_specs=(vmem,) * 4,
-        scratch_shapes=[
+        in_specs=[pl.BlockSpec(memory_space=pltpu.SMEM)] + [far] * (2 + len(consts)),
+        out_specs=(far,) * 4,
+        scratch_shapes=[pltpu.VMEM(m.shape, m.dtype) for m in consts] + [
+            pltpu.VMEM((3, za, ya, nx), f32),
+            pltpu.VMEM((3, zb, yb, nx), f32),
+            pltpu.VMEM((3, za, ya, nx), f32),
+            pltpu.VMEM((3, zb, yb, nx), f32),
             pltpu.VMEM((4, 3, za + 8, ya, nx), f32),
             pltpu.VMEM((4, 3, zb + 8, yb, nx), f32),
             pltpu.VMEM((3, za, ya, nx), f32),
@@ -295,8 +345,8 @@
             pltpu.VMEM((3, zb, yb, nx), f32),
             pltpu.VMEM(head_shape, f32),
             pltpu.VMEM(head_shape, f32),
-            pltpu.VMEM(head_shape, f32),
-            pltpu.VMEM(head_shape, f32),
+            pltpu.VMEM(coarse_shape, f32),
+            pltpu.VMEM(coarse_shape, f32),
             pltpu.VMEM((3, zb, yb, nx), f32),
             pltpu.SemaphoreType.DMA((4, 2, 2)),
             pltpu.SemaphoreType.DMA((4, 2, 2)),
@@ -304,9 +354,12 @@
             pltpu.SemaphoreType.DMA((2,)),
             pltpu.SemaphoreType.DMA((1 + 2 * exponents,)),
             pltpu.SemaphoreType.DMA((3,)),
+            pltpu.SemaphoreType.DMA((2,)),
+            pltpu.SemaphoreType.DMA((12,)),
+            pltpu.SemaphoreType.DMA((4,)),
         ],
         compiler_params=pltpu.CompilerParams(
-            collective_id=0, has_side_effects=True, vmem_limit_bytes=32 * 2**20),
+            collective_id=0, has_side_effects=True, vmem_limit_bytes=62 * 2**20),
     )(coeffs, grids_a, grids_b, *consts)
 
 

time: 60 us -> 45.6 us (0.76)
  local copies, waits for them, and re-layouts: 15.3 us -> 4.07 us
  Pallas kernels: 43.3 us -> 40.6 us
    unnamed x34 -> x10, local copies, waits for them, and re-layouts: 15.3 us -> 4.07 us
    pallas_call x1, Pallas kernels: 43.3 us -> 40.6 us  [shards(): pl.pallas_call(functools.partial(body, n, step, viscosity, space_a, space...]
where the time goes in v2:
time: 45.6 us; the launch traced here: 45.3 us
  Pallas kernels  40.6 us (89%)
  local copies, waits for them, and re-layouts  4.07 us (9%)
  between operations  0.65 us (1%)
    pallas_call x1, Pallas kernels, shards(): pl.pallas_call(functools.partial(body, n, step, viscosity, space_a, space...  40.6 us
    unnamed x10, local copies, waits for them, and re-layouts  4.07 us

profile of v2, /device:TPU:0, one launch (start us, length us, event | category | flops | bytes accessed | tf_op | source)
XLA Modules:
  0.0 45.3 jit_solution(2877608487820646112)
XLA Ops:
  0.6 40.6 %shard_map.174 = (f32[1,3,4,16,128]{4,3,2,1,0:T(8,128)}, f32[1,3,8,8,128]{4,3,2,1,0:T(8,128)}, f32[1,3,4,16,128]{4,3,2,1,0:T(8,128)}, f32[1,3,8,8,128]{4,3,2,1,0:T(8,128)}) custom-call(s32[4]{0:T(128)} %refs_0_.1, f32[1,3,4,16,128]{4,3,2,1,0:T(8,128)} %refs_1_.1, f32[1,3,8,8,128]{4,3,2,1,0:T(8,128)} %refs_2_.1, bf16[128,128]{1,0:T(8,128)(2,1)} %constant.24.clone.refs_3_, ...), custom_call_target="tpu_custom_call" | custom-call | tf_op jit(solution)/shard_map/pallas_call | solution.py:330
  41.2 0.0 copy-start.2
  41.2 1.6 %copy.23 = f32[1,3,4,16,128]{4,3,2,1,0:T(8,128)} copy(f32[1,3,4,16,128]{4,3,2,1,0:T(8,128)} %get-tuple-element.8) | data formatting | bytes 196608
  42.8 0.0 copy-done.2
  42.8 0.0 copy-start.1
  42.8 0.6 %copy.24 = f32[1,3,8,8,128]{4,3,2,1,0:T(8,128)} copy(f32[1,3,8,8,128]{4,3,2,1,0:T(8,128)S(1)} %copy-done.2) | data formatting | bytes 196608
  43.5 0.3 copy-done.1
  43.7 0.0 copy-start
  43.7 0.6 %copy.25 = f32[1,3,4,16,128]{4,3,2,1,0:T(8,128)} copy(f32[1,3,4,16,128]{4,3,2,1,0:T(8,128)S(1)} %copy-done.1) | data formatting | bytes 196608
  44.4 0.3 copy-done
  44.7 0.6 %copy.26 = f32[1,3,8,8,128]{4,3,2,1,0:T(8,128)} copy(f32[1,3,8,8,128]{4,3,2,1,0:T(8,128)S(1)} %copy-done) | data formatting | bytes 196608
Async XLA Ops:
  41.2 1.6 %copy-start.2 = (f32[1,3,8,8,128]{4,3,2,1,0:T(8,128)S(1)}, f32[1,3,8,8,128]{4,3,2,1,0:T(8,128)}, u32[]{:S(2)}) copy-start(f32[1,3,8,8,128]{4,3,2,1,0:T(8,128)} %get-tuple-element.9) | copy-start | bytes 294916
  42.8 0.9 %copy-start.1 = (f32[1,3,4,16,128]{4,3,2,1,0:T(8,128)S(1)}, f32[1,3,4,16,128]{4,3,2,1,0:T(8,128)}, u32[]{:S(2)}) copy-start(f32[1,3,4,16,128]{4,3,2,1,0:T(8,128)} %get-tuple-element.10) | copy-start | bytes 294916
  43.7 0.9 %copy-start = (f32[1,3,8,8,128]{4,3,2,1,0:T(8,128)S(1)}, f32[1,3,8,8,128]{4,3,2,1,0:T(8,128)}, u32[]{:S(2)}) copy-start(f32[1,3,8,8,128]{4,3,2,1,0:T(8,128)} %get-tuple-element.11) | copy-start | bytes 294916

commit v3 on v2

--- a/solution.py
+++ b/solution.py
@@ -312,6 +312,20 @@
         copy.wait()
 
 
+def hand_over(*refs):
+    count = 4
+    source, target, held, sems = refs[:count], refs[count : 2 * count], refs[2 * count : 3 * count], refs[3 * count]
+    loads = [pltpu.make_async_copy(source[i], held[i], sems.at[0, i]) for i in range(count)]
+    stores = [pltpu.make_async_copy(held[i], target[i], sems.at[1, i]) for i in range(count)]
+    for copy in loads:
+        copy.start()
+    for load, store in zip(loads, stores):
+        load.wait()
+        store.start()
+    for copy in stores:
+        copy.wait()
+
+
 def shards(n, grids_a, grids_b, coeffs):
     za, ya, nx = grids_a.shape[2:]
     zb, yb = grids_b.shape[2:4]
@@ -327,7 +341,7 @@
     far = pl.BlockSpec(memory_space=pltpu.HBM)
     shape_a = jax.ShapeDtypeStruct(grids_a.shape, f32)
     shape_b = jax.ShapeDtypeStruct(grids_b.shape, f32)
-    return pl.pallas_call(
+    results = pl.pallas_call(
         functools.partial(body, n, step, viscosity, space_a, space_b),
         out_shape=(shape_a, shape_b, shape_a, shape_b),
         in_specs=[pl.BlockSpec(memory_space=pltpu.SMEM)] + [far] * (2 + len(consts)),
@@ -361,6 +375,14 @@
         compiler_params=pltpu.CompilerParams(
             collective_id=0, has_side_effects=True, vmem_limit_bytes=62 * 2**20),
     )(coeffs, grids_a, grids_b, *consts)
+    return pl.pallas_call(
+        hand_over,
+        out_shape=(shape_a, shape_b, shape_a, shape_b),
+        in_specs=[far] * 4,
+        out_specs=(far,) * 4,
+        scratch_shapes=[pltpu.VMEM(r.shape, f32) for r in results] + [pltpu.SemaphoreType.DMA((2, 4))],
+        compiler_params=pltpu.CompilerParams(vmem_limit_bytes=62 * 2**20),
+    )(*results)
 
 
 def solution(mesh):

time: 45.6 us -> 43.2 us (0.947)
  local copies, waits for them, and re-layouts: 4.07 us -> 0 us
  Pallas kernels: 40.6 us -> 42.3 us
    unnamed x10 -> x0, local copies, waits for them, and re-layouts: 4.07 us -> none
    pallas_call x0 -> x1, Pallas kernels: none -> 1.75 us  [shards(): pl.pallas_call(hand_over, out_shape=(shape_a, shape_b, shape_a, shape_b),...]
where the time goes in v3:
time: 43.2 us; the launch traced here: 43 us
  Pallas kernels  42.3 us (98%)
  between operations  0.64 us (1%)
    pallas_call x1, Pallas kernels, shards(): pl.pallas_call(functools.partial(body, n, step, viscosity, space_a, space...  40.6 us
    pallas_call x1, Pallas kernels, shards(): pl.pallas_call(hand_over, out_shape=(shape_a, shape_b, shape_a, shape_b),...  1.75 us

profile of v3, /device:TPU:0, one launch (start us, length us, event | category | flops | bytes accessed | tf_op | source)
XLA Modules:
  0.0 43.0 jit_solution(15064130817557477207)
XLA Ops:
  0.6 40.6 %shard_map.174 = (f32[1,3,4,16,128]{4,3,2,1,0:T(8,128)}, f32[1,3,8,8,128]{4,3,2,1,0:T(8,128)}, f32[1,3,4,16,128]{4,3,2,1,0:T(8,128)}, f32[1,3,8,8,128]{4,3,2,1,0:T(8,128)}) custom-call(s32[4]{0:T(128)} %refs_0_.1, f32[1,3,4,16,128]{4,3,2,1,0:T(8,128)} %refs_1_.1, f32[1,3,8,8,128]{4,3,2,1,0:T(8,128)} %refs_2_.1, bf16[128,128]{1,0:T(8,128)(2,1)} %constant.24.clone.refs_3_, ...), custom_call_target="tpu_custom_call" | custom-call | tf_op jit(solution)/shard_map/pallas_call | solution.py:344
  41.2 1.7 %shard_map.175 = (f32[1,3,4,16,128]{4,3,2,1,0:T(8,128)}, f32[1,3,8,8,128]{4,3,2,1,0:T(8,128)}, f32[1,3,4,16,128]{4,3,2,1,0:T(8,128)}, f32[1,3,8,8,128]{4,3,2,1,0:T(8,128)}) custom-call(f32[1,3,4,16,128]{4,3,2,1,0:T(8,128)} %get-tuple-element.8.refs_0_, f32[1,3,8,8,128]{4,3,2,1,0:T(8,128)} %get-tuple-element.9.refs_1_, ...), custom_call_target="tpu_custom_call" | custom-call | tf_op jit(solution)/shard_map/pallas_call | solution.py:378
